TPU v7x, 32 devices: a whole 2x2x4 slice. The times are simulated.
32 devices in a mesh: fsdp: 4 (over y, x), ctx: 8 (over z, core).
Axes of the slice: x: 2, y: 2, z: 4, core: 2. Of those that a mesh axis runs over, the one named last changes fastest.
Arguments:
- tokens: bfloat16 [4, 1024, 1024], P('fsdp', 'ctx'), may hold values from -16 to 16
- cotangent: bfloat16 [4, 1024, 1024], P('fsdp', 'ctx'), may hold values from -6 to 6
- w_query: bfloat16 [1024, 512], P('fsdp')
- w_key: bfloat16 [1024, 512], P('fsdp')
- w_value: bfloat16 [1024, 512], P('fsdp'), may hold values from -0.1875 to 0.1875
- w_out: bfloat16 [512, 1024], P('fsdp'), may hold values from -0.25 to 0.25
- block_mask: int32 [8, 8], replicated, may hold values from 0 to 1, as said below
- span_order: int32 [16], replicated, may hold values from 0 to 15, each once
Outputs:
- mixed_out: bfloat16 [4, 1024, 1024], P('fsdp', 'ctx')
- token_grad: bfloat16 [4, 1024, 1024], P('fsdp', 'ctx')
- grad_query: float32 [1024, 512], P(('fsdp', 'ctx'))
- grad_key: float32 [1024, 512], P(('fsdp', 'ctx'))
- grad_value: float32 [1024, 512], P(('fsdp', 'ctx'))
- grad_out: float32 [512, 1024], P(('fsdp', 'ctx'))
Inputs may be any that keep to these rules, and one draw needn't show every extreme that they name: `block_mask`: every diagonal entry is 1.
All inputs are finite; a program needn't handle non-finite values.
Results may differ from a plain program's by a relative error of at most 0.013.
The roundings to bfloat16 on the way count: a program that leaves them out, or rounds other values in their place, can miss the bound.
Values may be sent and summed in bfloat16 or wider, within the bound.
A program may use at most 128 MiB of HBM per device.

v0:
```python
import math

import jax
import jax.numpy as jnp
from jax import lax
from jax.sharding import PartitionSpec as P

HEADS = 4
HD = 128
BLK = 128
SPAN = 64


NEG = -1e30
HIGH = lax.Precision.HIGHEST


def block_ids(span_order, start, count):
    rows = start + jnp.arange(count, dtype=jnp.int32)
    span = rows // SPAN
    lanes = jnp.arange(span_order.shape[0], dtype=jnp.int32)
    first = jnp.sum(jnp.where(span[:, None] == lanes[None, :], span_order[None, :], 0), axis=1)
    return (first * SPAN + rows % SPAN) // BLK


def allowed_between(mask_f, row_ids, col_ids):
    lanes = jnp.arange(mask_f.shape[0], dtype=jnp.int32)
    left = (row_ids[:, None] == lanes[None, :]).astype(jnp.float32)
    right = (col_ids[:, None] == lanes[None, :]).astype(jnp.float32)
    linked = jnp.dot(jnp.dot(left, mask_f), right.T)
    return linked > 0.5


def over_blocks(step, carry, pieces):
    count = pieces[0].shape[0]
    width = 512
    stacked = tuple((piece.reshape((count // width, width) + piece.shape[1:]) for piece in pieces))

    def scan_step(state, item):
        number, parts = item
        return (step(state, parts, number * width), None)

    numbers = jnp.arange(count // width, dtype=jnp.int32)
    carry, _ = lax.scan(scan_step, carry, (numbers, stacked))
    return carry


def contract_rows(left, right):
    return lax.dot_general(
        left, right, (((0,), (0,)), ((), ())), preferred_element_type=jnp.float32
    )


def contract_cols(left, right):
    return lax.dot_general(
        left, right, (((1,), (1,)), ((), ())), preferred_element_type=jnp.float32
    )


def body(tokens, cotangent, w_query, w_key, w_value, w_out, block_mask, span_order):
    x_rows = tokens[0]
    dy_rows = cotangent[0]
    rows = x_rows.shape[0]
    scale = 1.0 / math.sqrt(HD)
    full_q, full_k, full_v, full_o = (
        lax.all_gather(w_query, "fsdp", axis=0, tiled=True),
        lax.all_gather(w_key, "fsdp", axis=0, tiled=True),
        lax.all_gather(w_value, "fsdp", axis=0, tiled=True),
        lax.all_gather(w_out, "fsdp", axis=0, tiled=True),
    )
    query = jnp.dot(x_rows, full_q, preferred_element_type=jnp.float32).astype(jnp.bfloat16)
    keys = jnp.dot(x_rows, full_k, preferred_element_type=jnp.float32).astype(jnp.bfloat16)
    values = jnp.dot(x_rows, full_v, preferred_element_type=jnp.float32).astype(jnp.bfloat16)
    d_attn = contract_cols(dy_rows, full_o).astype(jnp.bfloat16)
    mask_f = block_mask.astype(jnp.float32)
    own_ids = block_ids(span_order, lax.axis_index("ctx") * rows, rows)
    q_own = query.reshape(rows, HEADS, HD)
    k_own = keys.reshape(rows, HEADS, HD)
    v_own = values.reshape(rows, HEADS, HD)
    g_own = d_attn.reshape(rows, HEADS, HD)

    def sweep_keys(carry, parts, start):
        top, total, out_acc, mix_acc, key_acc, dot_acc = carry
        count = parts[0].shape[0]
        k_part = parts[0].reshape(count, HEADS, HD)
        v_part = parts[1].reshape(count, HEADS, HD)
        keep = allowed_between(mask_f, own_ids, block_ids(span_order, start, count))[None]
        score = (
            jnp.einsum("qhd,khd->hqk", q_own, k_part, preferred_element_type=jnp.float32) * scale
        )
        score = jnp.where(keep, score, NEG)
        new_top = jnp.maximum(top, jnp.max(score, axis=-1))
        fade = jnp.exp(top - new_top)
        prob = jnp.where(keep, jnp.exp(score - new_top[:, :, None]), 0.0)
        k_wide = k_part.astype(jnp.float32)
        v_wide = v_part.astype(jnp.float32)
        total = fade * total + jnp.sum(prob, axis=-1)
        out_acc = fade[:, :, None] * out_acc + jnp.einsum(
            "hqk,khd->hqd", prob, v_wide, precision=HIGH
        )
        d_prob = jnp.einsum("qhd,khd->hqk", g_own, v_part, preferred_element_type=jnp.float32)
        weighted = prob * d_prob
        dot_acc = fade * dot_acc + jnp.sum(weighted, axis=-1)
        mix_acc = fade[:, :, None] * mix_acc + jnp.einsum(
            "hqk,khd->hqd", weighted, k_wide, precision=HIGH
        )
        key_acc = fade[:, :, None] * key_acc + jnp.einsum(
            "hqk,khd->hqd", prob, k_wide, precision=HIGH
        )
        return (new_top, total, out_acc, mix_acc, key_acc, dot_acc)

    flat = jnp.zeros((HEADS, rows), jnp.float32)
    cube = jnp.zeros((HEADS, rows, HD), jnp.float32)
    begin = (jnp.full((HEADS, rows), NEG, jnp.float32), flat, cube, cube, cube, flat)
    top, total, out_acc, mix_acc, key_acc, dot_acc = over_blocks(
        sweep_keys,
        begin,
        (
            lax.all_gather(keys, "ctx", axis=0, tiled=True),
            lax.all_gather(values, "ctx", axis=0, tiled=True),
        ),
    )
    share = 1.0 / total
    combined = out_acc * share[:, :, None]
    log_total = top + jnp.log(total)
    attention = jnp.transpose(combined, (1, 0, 2)).reshape(rows, HEADS * HD).astype(jnp.bfloat16)
    mixed = (
        x_rows.astype(jnp.float32) + jnp.dot(attention, full_o, preferred_element_type=jnp.float32)
    ).astype(jnp.bfloat16)
    delta = dot_acc * share
    log_rows = jnp.transpose(log_total)
    delta_rows = jnp.transpose(delta)

    def key_side(acc, parts, start):
        d_key, d_value = acc
        count = parts[0].shape[0]
        q_part = parts[0].reshape(count, HEADS, HD)
        g_part = parts[1].reshape(count, HEADS, HD)
        lse_part = jnp.transpose(parts[2])
        delta_part = jnp.transpose(parts[3])
        keep = allowed_between(mask_f, block_ids(span_order, start, count), own_ids)[None]
        score = (
            jnp.einsum("khd,qhd->hkq", q_part, k_own, preferred_element_type=jnp.float32) * scale
        )
        score = jnp.where(keep, score, NEG)
        prob = jnp.where(keep, jnp.exp(score - lse_part[:, :, None]), 0.0)
        d_prob = jnp.einsum("khd,qhd->hkq", g_part, v_own, preferred_element_type=jnp.float32)
        d_score = prob * (d_prob - delta_part[:, :, None])
        d_key = d_key + scale * jnp.einsum(
            "hkq,khd->hqd", d_score, q_part.astype(jnp.float32), precision=HIGH
        )
        d_value = d_value + jnp.einsum(
            "hkq,khd->hqd", prob, g_part.astype(jnp.float32), precision=HIGH
        )
        return (d_key, d_value)

    d_query = scale * (mix_acc - delta[:, :, None] * key_acc) * share[:, :, None]
    d_key, d_value = over_blocks(
        key_side,
        (cube, cube),
        (
            lax.all_gather(query.astype(jnp.float32), "ctx", axis=0, tiled=True).astype(
                jnp.bfloat16
            ),
            lax.all_gather(d_attn.astype(jnp.float32), "ctx", axis=0, tiled=True).astype(
                jnp.bfloat16
            ),
            lax.all_gather(log_rows, "ctx", axis=0, tiled=True),
            lax.all_gather(delta_rows, "ctx", axis=0, tiled=True),
        ),
    )

    def to_rows(grad_heads):
        return jnp.transpose(grad_heads, (1, 0, 2)).reshape(rows, HEADS * HD).astype(jnp.bfloat16)

    dq_rows = to_rows(d_query)
    dk_rows = to_rows(d_key)
    dv_rows = to_rows(d_value)
    token_grad = (
        dy_rows.astype(jnp.float32)
        + contract_cols(dq_rows, full_q)
        + contract_cols(dk_rows, full_k)
        + contract_cols(dv_rows, full_v)
    ).astype(jnp.bfloat16)
    grad_q = contract_rows(x_rows, dq_rows)
    grad_k = contract_rows(x_rows, dk_rows)
    grad_v = contract_rows(x_rows, dv_rows)
    grad_o = contract_rows(attention, dy_rows)
    grad_q, grad_k, grad_v, grad_o = (
        lax.psum_scatter(grad_q, ("fsdp", "ctx"), scatter_dimension=0, tiled=True),
        lax.psum_scatter(grad_k, ("fsdp", "ctx"), scatter_dimension=0, tiled=True),
        lax.psum_scatter(grad_v, ("fsdp", "ctx"), scatter_dimension=0, tiled=True),
        lax.psum_scatter(grad_o, ("fsdp", "ctx"), scatter_dimension=0, tiled=True),
    )
    return (mixed[None], token_grad[None], grad_q, grad_k, grad_v, grad_o)


def solution(mesh):
    return jax.shard_map(
        body,
        mesh=mesh,
        in_specs=(
            P("fsdp", "ctx", None),
            P("fsdp", "ctx", None),
            P("fsdp", None),
            P("fsdp", None),
            P("fsdp", None),
            P("fsdp", None),
            P(),
            P(),
        ),
        out_specs=(
            P("fsdp", "ctx", None),
            P("fsdp", "ctx", None),
            P(("fsdp", "ctx"), None),
            P(("fsdp", "ctx"), None),
            P(("fsdp", "ctx"), None),
            P(("fsdp", "ctx"), None),
        ),
        check_vma=False,
    )
```

profile of v0, /device:TPU:0, one launch (start us, length us, event | category | flops | bytes accessed | tf_op | source)
XLA Modules:
  0.0 787.3 jit_solution(11975900808611746219)
XLA Ops:
  7.2 0.7 all-gather.9.cloned.1.call-update
  8.0 0.7 all-gather.15.cloned.1.call-update
  8.7 0.7 all-gather.19.cloned.1.call-update
  9.5 0.5 all-gather.13.cloned.1.call-update
  10.1 29.2 %all-gather.9.cloned.1.call-done = bf16[1024,512]{1,0:T(8,128)(2,1)} async-done(((bf16[256,512]{1,0:T(8,128)(2,1)}), bf16[1024,512]{1,0:T(8,128)(2,1)}) %all-gather.9.cloned.1.call-update) | async-done | bytes 1048592 | tf_op jit(solution)/shard_map/all_gather | solution.py:67
  39.2 2.3 convolution_convert_fusion.3
  41.6 26.1 %all-gather.15.cloned.1.call-done = bf16[1024,512]{1,0:T(8,128)(2,1)} async-done(((bf16[256,512]{1,0:T(8,128)(2,1)}), bf16[1024,512]{1,0:T(8,128)(2,1)}) %all-gather.15.cloned.1.call-update) | async-done | bytes 1048592 | tf_op jit(solution)/shard_map/all_gather | solution.py:68
  67.7 2.2 convolution_convert_fusion.1
  70.0 26.2 %all-gather.19.cloned.1.call-done = bf16[512,1024]{1,0:T(8,128)(2,1)} async-done(((bf16[128,1024]{1,0:T(8,128)(2,1)}), bf16[512,1024]{1,0:T(8,128)(2,1)}) %all-gather.19.cloned.1.call-update) | async-done | bytes 1048592 | tf_op jit(solution)/shard_map/all_gather | solution.py:69
  96.2 2.4 convolution_convert_fusion
  98.9 1.6 copy_bitcast_fusion.2
  100.5 0.7 copy_bitcast_fusion
  101.2 0.7 copy_bitcast_fusion.1
  101.9 22.7 %all-gather.13.cloned.1.call-done = bf16[1024,512]{1,0:T(8,128)(2,1)} async-done(((bf16[256,512]{1,0:T(8,128)(2,1)}), bf16[1024,512]{1,0:T(8,128)(2,1)}) %all-gather.13.cloned.1.call-update) | async-done | bytes 1048592 | tf_op jit(solution)/shard_map/all_gather | solution.py:66
  124.6 1.5 convolution_convert_fusion.2
  126.1 0.7 copy_bitcast_fusion.3
  126.9 21.2 %all-gather.11.cloned.1.call-done = bf16[1024,512]{1,0:T(8,128)(2,1)} async-done(((bf16[128,512]{1,0:T(8,128)(2,1)}), bf16[1024,512]{1,0:T(8,128)(2,1)}) %all-gather.11.cloned.1.call-update) | async-done | bytes 1048592 | tf_op jit(solution)/shard_map/all_gather | solution.py:119
  148.2 23.2 %all-gather.17.cloned.1.call-done = bf16[1024,512]{1,0:T(8,128)(2,1)} async-done(((bf16[128,512]{1,0:T(8,128)(2,1)}), bf16[1024,512]{1,0:T(8,128)(2,1)}) %all-gather.17.cloned.1.call-update) | async-done | bytes 1048592 | tf_op jit(solution)/shard_map/all_gather | solution.py:120
  171.4 20.9 %while.40 = (s32[]{:T(128)}, f32[4,128]{1,0:T(4,128)S(1)}, f32[4,128]{1,0:T(4,128)S(1)}, f32[4,128,128]{2,1,0:T(8,128)}, f32[4,128,128]{2,1,0:T(8,128)}, /*index...) while((s32[]{:T(128)}, f32[4,128]{1,0:T(4,128)S(1)}, ...), condition=%wide.region_6.7_spmd.clone, body=%wide.region_1.6_spmd.clone.sunk | while | flops 1347623424 | bytes 22871104 | solution.py:44
  171.4 0.6 dynamic_slice.79
  172.7 0.5 convolution_compare_fusion.4
  173.4 1.3 constant_dynamic-slice_fusion.6
  174.9 1.3 fusion.129
  176.5 1.4 fusion.131
  177.9 1.1 convolution_add_fusion.14
  179.0 1.0 convolution_add_fusion.13
  180.1 1.1 convolution_add_fusion.12
  181.9 0.6 dynamic_slice.79
  183.2 0.5 convolution_compare_fusion.4
  183.9 1.3 constant_dynamic-slice_fusion.6
  185.4 1.3 fusion.129
  186.9 1.4 fusion.131
  188.4 1.1 convolution_add_fusion.14
  189.5 1.0 convolution_add_fusion.13
  190.5 1.1 convolution_add_fusion.12
  192.3 0.6 fusion.50
  192.9 12.7 %all_gather.39 = f32[1024,4]{0,1:T(4,128)S(1)} all-gather(f32[128,4]{0,1:T(4,128)S(1)} %bitcast.203), channel_id=1, replica_groups=mesh['fsdp'=4,'ctx'=8] {'ctx'}, dimensions={0}, use_global_device_ids=true | all-gather | bytes 18432 | tf_op jit(solution)/shard_map/all_gather | solution.py:169
  205.6 13.0 %all_gather.37 = f32[1024,4]{0,1:T(4,128)S(1)} all-gather(f32[128,4]{0,1:T(4,128)S(1)} %get-tuple-element.754), channel_id=1, replica_groups=mesh['fsdp'=4,'ctx'=8] {'ctx'}, dimensions={0}, use_global_device_ids=true | all-gather | bytes 18432 | tf_op jit(solution)/shard_map/all_gather | solution.py:168
  218.6 14.8 %while.41 = (s32[]{:T(128)}, f32[4,128,128]{2,1,0:T(8,128)S(1)}, f32[4,128,128]{2,1,0:T(8,128)S(1)}, s32[2]{0:T(128)S(1)}, s32[16]{0:T(128)S(1)}, /*index=5*/bf1...) while((s32[]{:T(128)}, f32[4,128,128]{2,1,0:T(8,128)S(1)}, ...), condition=%wide.region_9.10_spmd.clone, body=%wide.region_7.9_spmd.clone.sunk | while | flops 942656512 | bytes 14354712 | solution.py:44
  218.7 0.7 dynamic_slice.82
  220.1 0.5 convolution_compare_fusion.5
  220.7 1.3 constant_dynamic-slice_fusion.7
  222.2 0.7 fusion.144
  223.2 1.0 convolution_add_fusion.15
  224.8 1.1 fusion.146
  226.1 0.7 dynamic_slice.82
  227.5 0.5 convolution_compare_fusion.5
  228.1 1.3 constant_dynamic-slice_fusion.7
  229.6 0.7 fusion.144
  230.6 1.0 convolution_add_fusion.15
  231.6 0.5 fusion.145
  232.2 1.1 fusion.146
  233.9 1.8 copy.133
  236.4 1.8 copy.135
  238.3 0.9 copy-done.6
  239.9 1.9 copy.131
  241.9 0.9 copy-done.3
  242.9 1.8 fusion.40
  244.8 1.0 fusion.39
  247.3 1.2 fusion.38
  248.5 123.3 %reduce-scatter.15.cloned.1.call-done = f32[32,512]{1,0:T(8,128)} async-done(((f32[1024,512]{1,0:T(8,128)}), f32[32,512]{1,0:T(8,128)}) %reduce-scatter.15.cloned.1.call-update) | async-done | bytes 65552
  371.8 135.8 %reduce-scatter.17.cloned.1.call-done = f32[32,512]{1,0:T(8,128)} async-done(((f32[1024,512]{1,0:T(8,128)}), f32[32,512]{1,0:T(8,128)}) %reduce-scatter.17.cloned.1.call-update) | async-done | bytes 65552
  507.6 136.2 %reduce-scatter.13.cloned.1.call-done = f32[32,512]{1,0:T(8,128)} async-done(((f32[1024,512]{1,0:T(8,128)}), f32[32,512]{1,0:T(8,128)}) %reduce-scatter.13.cloned.1.call-update) | async-done | bytes 65552
  643.8 136.7 %reduce-scatter.11.cloned.1.call-done = f32[16,1024]{1,0:T(8,128)} async-done(((f32[512,1024]{1,0:T(8,128)}), f32[16,1024]{1,0:T(8,128)}) %reduce-scatter.11.cloned.1.call-update) | async-done | bytes 65552 | tf_op jit(solution)/shard_map/reduce_scatter | solution.py:193
  (186 shorter events, 8.8 us)
Async XLA Ops:
  7.2 60.6 %copy-start = (bf16[1,128,1024]{2,1,0:T(8,128)(2,1)S(1)}, bf16[1,128,1024]{2,1,0:T(8,128)(2,1)}, u32[]{:S(2)}) copy-start(bf16[1,128,1024]{2,1,0:T(8,128)(2,1)} %param.12) | copy-start | bytes 786436
  7.2 89.1 %copy-start.15 = (bf16[1,128,1024]{2,1,0:T(8,128)(2,1)S(1)}, bf16[1,128,1024]{2,1,0:T(8,128)(2,1)}, u32[]{:S(2)}) copy-start(bf16[1,128,1024]{2,1,0:T(8,128)(2,1)} %param.13) | copy-start | bytes 786436
  7.2 32.0 %all-gather.9.cloned.1.call-start = ((), (), s32[]{:S(2)}) async-start(), calls=%async_computation.4 | async-start | bytes 1310720 | tf_op jit(solution)/shard_map/all_gather | solution.py:67
  7.9 59.8 %all-gather.15.cloned.1.call-start = ((), (), s32[]{:S(2)}) async-start(), calls=%async_computation.7 | async-start | bytes 1310720 | tf_op jit(solution)/shard_map/all_gather | solution.py:68
  8.7 87.6 %all-gather.19.cloned.1.call-start = ((), (), s32[]{:S(2)}) async-start(), calls=%async_computation.9 | async-start | bytes 1310720 | tf_op jit(solution)/shard_map/all_gather | solution.py:69
  9.4 115.2 %all-gather.13.cloned.1.call-start = ((), (), s32[]{:S(2)}) async-start(), calls=%async_computation.6 | async-start | bytes 1310720 | tf_op jit(solution)/shard_map/all_gather | solution.py:66
  10.0 88.8 %copy-start.27 = (s32[8,8]{1,0:T(8,128)S(1)}, s32[8,8]{1,0:T(8,128)}, u32[]{:S(2)}) copy-start(s32[8,8]{1,0:T(8,128)} %param.18) | copy-start | bytes 772
  10.0 88.8 %copy-start.25 = (s32[16]{0:T(128)S(1)}, s32[16]{0:T(128)}, u32[]{:S(2)}) copy-start(s32[16]{0:T(128)} %param.19) | copy-start | bytes 196
  10.0 138.2 %all-gather.11.cloned.1.call-start = ((), (), s32[]{:S(2)}) async-start(), calls=%async_computation.5 | async-start | bytes 1179648 | tf_op jit(solution)/shard_map/all_gather | solution.py:119
  41.5 59.7 %copy-start.18 = (bf16[128,512]{1,0:T(8,128)(2,1)S(1)}, bf16[128,512]{1,0:T(8,128)(2,1)}, u32[]{:S(2)}) copy-start(bf16[128,512]{1,0:T(8,128)(2,1)} %convolution_convert_fusion.3) | copy-start | bytes 393220
  41.5 129.8 %all-gather.17.cloned.1.call-start = ((), (), s32[]{:S(2)}) async-start(), calls=%async_computation.8 | async-start | bytes 1179648 | tf_op jit(solution)/shard_map/all_gather | solution.py:120
  69.9 30.6 %copy-start.19 = (bf16[128,512]{1,0:T(8,128)(2,1)S(1)}, bf16[128,512]{1,0:T(8,128)(2,1)}, u32[]{:S(2)}) copy-start(bf16[128,512]{1,0:T(8,128)(2,1)} %convolution_convert_fusion.1) | copy-start | bytes 393220
  69.9 148.7 %all-gather.23.cloned.1.call-start = ((), (), s32[]{:S(2)}) async-start(), calls=%async_computation.11 | async-start | bytes 1179648 | tf_op jit(solution)/shard_map/all_gather | solution.py:165
  98.7 119.9 %all-gather.21.cloned.1.call-start = ((), (), s32[]{:S(2)}) async-start(), calls=%async_computation.10 | async-start | bytes 1179648 | tf_op jit(solution)/shard_map/all_gather | solution.py:162
  126.1 0.7 copy-start.17
  126.9 244.9 %reduce-scatter.15.cloned.1.call-start = ((), (), s32[]{:S(2)}) async-start(), calls=%async_computation.14 | async-start | bytes 2162688
  176.4 1.5 copy-start.4
  176.5 2.5 copy-start.7
  177.9 2.2 copy-start.1
  179.0 2.2 copy-start.5
  180.0 1.4 copy-start.8
  181.1 0.7 copy-start.2
  186.9 1.4 copy-start.4
  186.9 2.5 copy-start.7
  188.4 2.2 copy-start.1
  189.5 2.2 copy-start.5
  190.5 1.4 copy-start.8
  191.6 0.7 copy-start.2
  218.6 3.6 copy-start.20
  218.6 3.6 copy-start.22
  218.6 3.6 copy-start.28
  218.6 3.6 copy-start.30
  218.6 3.6 copy-start.32
  218.6 3.6 copy-start.24
  223.0 1.3 copy-start.10
  224.7 1.2 copy-start.21
  224.8 1.2 copy-start.23
  224.8 1.2 copy-start.29
  224.8 1.2 copy-start.31
  224.8 1.2 copy-start.33
  226.0 3.6 copy-start.20
  226.0 3.6 copy-start.22
  226.0 3.6 copy-start.28
  226.0 3.6 copy-start.30
  226.0 3.6 copy-start.32
  226.0 3.6 copy-start.24
  230.4 1.3 copy-start.10
  232.1 1.2 copy-start.21
  232.2 1.2 copy-start.23
  232.2 1.2 copy-start.29
  232.2 1.2 copy-start.31
  232.2 1.2 copy-start.33
  235.8 271.8 %reduce-scatter.17.cloned.1.call-start = ((), (), s32[]{:S(2)}) async-start(), calls=%async_computation.15 | async-start | bytes 2162688
  238.2 0.9 copy-start.6
  238.2 1.1 copy-start.9
  238.2 1.2 copy-start.26
  238.3 405.5 %reduce-scatter.13.cloned.1.call-start = ((), (), s32[]{:S(2)}) async-start(), calls=%async_computation.13 | async-start | bytes 2162688
  241.8 0.9 copy-start.3
  241.8 1.1 copy-start.16
  241.8 538.6 %reduce-scatter.11.cloned.1.call-start = ((), (), s32[]{:S(2)}) async-start(), calls=%async_computation.12 | async-start | bytes 2162688 | tf_op jit(solution)/shard_map/reduce_scatter | solution.py:193
  242.9 1.9 copy-start.13
  244.8 1.2 copy-start.14
  244.8 1.7 copy-start.11
  246.0 1.3 copy-start.12
Sparse Core Ops, SparseCore 0:
  9.9 29.3 all-gather.8
  41.1 26.6 all-gather.14
  69.6 26.6 all-gather.18
  97.9 26.6 all-gather.12
  126.0 22.0 all-gather.10
  149.6 21.7 all-gather.16
  173.0 21.6 all-gather.22
  196.2 21.7 all-gather.20
  235.9 135.8 reduce-scatter.14
  374.6 133.0 reduce-scatter.16
  510.5 133.2 reduce-scatter.12
  646.6 133.8 reduce-scatter.10
where the time goes:
time: 788 us; the launch traced here: 787 us
  waiting for transfers between devices  683 us (87%)
  matrix products  35.1 us (4%)
  blocking collectives  25.7 us (3%)
  local copies, waits for them, and re-layouts  22.8 us (3%)
  between operations  14.5 us (2%)
    unnamed x15, waiting for transfers between devices  398 us
    reduce_scatter x1, waiting for transfers between devices, body(): lax.psum_scatter(grad_o, ('fsdp', 'ctx'), scatter_dimension=0, tiled=True)  137 us
    all_gather x1, waiting for transfers between devices, body(): lax.all_gather(w_key, 'fsdp', axis=0, tiled=True)  29.2 us
    all_gather x1, waiting for transfers between devices, body(): lax.all_gather(w_out, 'fsdp', axis=0, tiled=True)  26.2 us
    all_gather x1, waiting for transfers between devices, body(): lax.all_gather(w_value, 'fsdp', axis=0, tiled=True)  26.1 us
    all_gather x1, waiting for transfers between devices, body(): lax.all_gather(values, 'ctx', axis=0, tiled=True)  23.2 us
    all_gather x1, waiting for transfers between devices, body(): lax.all_gather(w_query, 'fsdp', axis=0, tiled=True)  22.7 us
    all_gather x1, waiting for transfers between devices, body(): lax.all_gather(keys, 'ctx', axis=0, tiled=True)  21.2 us
  transfers between devices with their start and end apart: 12, of which 10 were waited for; matrix products, arithmetic and copies ran while one was open for 5% of the time, Pallas kernels for 0%

commit v1 on v0

--- a/solution.py
+++ b/solution.py
@@ -1,8 +1,11 @@
+import functools
 import math
 
 import jax
 import jax.numpy as jnp
 from jax import lax
+from jax.experimental import pallas as pl
+from jax.experimental.pallas import tpu as pltpu
 from jax.sharding import PartitionSpec as P
 
 HEADS = 4
@@ -195,9 +198,339 @@
     return (mixed[None], token_grad[None], grad_q, grad_k, grad_v, grad_o)
 
 
+def dot_rows(left, right):
+    return lax.dot_general(
+        left, right, (((0,), (0,)), ((), ())), preferred_element_type=jnp.float32
+    )
+
+
+def dot_plain(left, right):
+    return jnp.dot(left, right, preferred_element_type=jnp.float32)
+
+
+def fused_kernel(
+    F,
+    x_ref, dy_ref, wq_ref, wk_ref, wv_ref, wo_ref, bias_ref,
+    mixed_ref, token_ref, gq_ref, gk_ref, gv_ref, go_ref,
+    xg, wq_all, wk_all, wv_all, wo_all, wh, g_send, g_got, kv_buf, q_buf,
+    att_send, att_own, dq_send, dq_own, dkv_acc, dkv_pair, dkv_send, dkv_own, d_head,
+    go0, go0_got, go1, go1_got, go2, go2_got,
+    gw0, gw0_got, gw1, gw1_got, gw2, gw2_got,
+    x_s, x_r, xf_s, xf_r, w_s, w_r, wf_s, wf_r, g_s, g_r, at_s, at_r, dq_s, dq_r,
+    dk_s, dk_r, pair_s, pair_r, go1_s, go1_r, go2_s, go2_r, gw1_s, gw1_r, gw2_s, gw2_r,
+):
+    H = HEADS
+    f = lax.axis_index("fsdp")
+    ctx = lax.axis_index("ctx")
+    z = ctx // 2
+    c = ctx % 2
+    other = 1 - c
+    rows = x_ref.shape[0]
+    bf = jnp.bfloat16
+    f32 = jnp.float32
+    scale = 1.0 / math.sqrt(HD)
+
+    pair_dev = (f, z * 2 + other)
+
+    def head_dev(k):
+        return (f, lax.rem(z + k, H) * 2 + c)
+
+    def clip_dev(k):
+        return (lax.rem(f + k, F), ctx)
+
+    started = []
+
+    def send(src, dst, s, r, dev):
+        copy = pltpu.make_async_remote_copy(
+            src_ref=src, dst_ref=dst, send_sem=s, recv_sem=r,
+            device_id=dev, device_id_type=pl.DeviceIdType.MESH,
+        )
+        copy.start()
+        started.append(copy)
+        return copy
+
+    barrier = pltpu.get_barrier_semaphore()
+    peers = [pair_dev] + [head_dev(k) for k in range(1, H)] + [clip_dev(k) for k in range(1, F)]
+    for dev in peers:
+        pl.semaphore_signal(barrier, inc=1, device_id=dev, device_id_type=pl.DeviceIdType.MESH)
+    pl.semaphore_wait(barrier, len(peers))
+
+    weights = ((wo_ref, wo_all), (wk_ref, wk_all), (wv_ref, wv_all), (wq_ref, wq_all))
+
+    def half_of(i, owner, part):
+        n = weights[i][0].shape[0]
+        start = pl.multiple_of(owner * n + part * (n // 2), n // 2)
+        return weights[i][1].at[pl.ds(start, n // 2)]
+
+    def w_send(i):
+        ref = weights[i][0]
+        n = ref.shape[0] // 2
+        src = ref.at[pl.ds(pl.multiple_of(c * n, n), n)]
+        return [
+            send(src, half_of(i, f, c), w_s.at[i, k - 1], w_r.at[i, k - 1], clip_dev(k))
+            for k in range(1, F)
+        ]
+
+    w_copies = [w_send(0)]
+    x_copies = [
+        send(x_ref, xg.at[c, z], x_s.at[k - 1], x_r.at[k - 1], head_dev(k)) for k in range(1, H)
+    ]
+    x_pair = [send(x_ref, xg.at[c, z], xf_s.at[0], xf_r.at[0], pair_dev)]
+    for i in range(1, 4):
+        w_copies.append(w_send(i))
+
+    xg[c, z] = x_ref[...]
+    for ref, whole in weights:
+        n = ref.shape[0]
+        whole[pl.ds(pl.multiple_of(f * n, n), n), :] = ref[...]
+
+    def w_forward(i):
+        out = []
+        for k in range(1, F):
+            w_copies[i][k - 1].wait_recv()
+            part = half_of(i, lax.rem(f + F - k, F), c)
+            out.append(send(part, part, wf_s.at[i, k - 1], wf_r.at[i, k - 1], pair_dev))
+        return out
+
+    def x_forward(k):
+        x_copies[k - 1].wait_recv()
+        part = xg.at[c, lax.rem(z + H - k, H)]
+        x_pair.append(send(part, part, xf_s.at[k], xf_r.at[k], pair_dev))
+
+    for copy in w_forward(0):
+        copy.wait_recv()
+    g_all = lax.dot_general(
+        dy_ref[...], wo_all[...], (((1,), (1,)), ((), ())), preferred_element_type=f32
+    ).astype(bf)
+    for h in range(H):
+        g_send[h] = g_all[:, h * HD:(h + 1) * HD]
+    g_copies = []
+    for k in range(1, H):
+        to = lax.rem(z + k, H)
+        g_copies.append(send(g_send.at[to], g_got.at[z], g_s.at[k - 1], g_r.at[k - 1], head_dev(k)))
+    g_got[z] = g_send[z]
+
+    forwards = []
+    forwards += w_forward(1)
+    x_forward(1)
+    forwards += w_forward(2)
+    x_forward(3)
+    x_forward(2)
+    forwards += w_forward(3)
+    for copy in forwards:
+        copy.wait_recv()
+    cols = pl.ds(pl.multiple_of(z * HD, HD), HD)
+    wh[:, :HD] = wk_all[:, cols]
+    wh[:, HD:2 * HD] = wv_all[:, cols]
+    wh[:, 2 * HD:] = wq_all[:, cols]
+    own_x = xg[c].reshape(H * rows, -1)
+    own_kvq = dot_plain(own_x, wh[...]).astype(bf)
+    kv_buf[c] = own_kvq[:, :2 * HD]
+    for h in range(H):
+        q_buf[h] = own_kvq[h * rows:(h + 1) * rows, 2 * HD:]
+    for copy in x_pair:
+        copy.wait_recv()
+    kv_buf[other] = dot_plain(xg[other].reshape(H * rows, -1), wh[:, :2 * HD]).astype(bf)
+    for copy in g_copies:
+        copy.wait_recv()
+
+    kv = kv_buf[...].reshape(2 * H * rows, 2 * HD)
+    keys = kv[:, :HD]
+    values = kv[:, HD:]
+    spans = rows // SPAN
+    at_copies, dq_copies = [], []
+    for k in (1, 2, 3, 0):
+        h = lax.rem(z + k, H)
+        query = q_buf[h]
+        grad = g_got[h]
+        score = contract_cols(query, keys) * scale
+        line = bias_ref[c, h]
+        score = score + jnp.concatenate(
+            [jnp.broadcast_to(line[s:s + 1], (SPAN, line.shape[1])) for s in range(spans)], axis=0
+        )
+        prob = jnp.exp(score - jnp.max(score, axis=1, keepdims=True))
+        prob = prob * (1.0 / jnp.sum(prob, axis=1, keepdims=True))
+        prob_b = prob.astype(bf)
+        att = dot_plain(prob_b, values).astype(bf)
+        att_send[h] = att
+        if k == 0:
+            att_own[:, cols] = att
+        else:
+            at_copies.append(send(
+                att_send.at[h], att_own.at[:, cols], at_s.at[k - 1], at_r.at[k - 1], head_dev(k)
+            ))
+        d_prob = contract_cols(grad, values)
+        delta = jnp.sum(prob * d_prob, axis=1, keepdims=True)
+        d_score = (prob * (d_prob - delta) * scale).astype(bf)
+        d_query = dot_plain(d_score, keys).astype(bf)
+        dq_send[h] = d_query
+        if k == 0:
+            dq_own[:, cols] = d_query
+        else:
+            dq_copies.append(send(
+                dq_send.at[h], dq_own.at[:, cols], dq_s.at[k - 1], dq_r.at[k - 1], head_dev(k)
+            ))
+        d_key = dot_rows(d_score, query).reshape(2, H * rows, HD)
+        d_value = dot_rows(prob_b, grad).reshape(2, H * rows, HD)
+        if k == 1:
+            dkv_acc[:, :, :HD] = d_key
+            dkv_acc[:, :, HD:] = d_value
+        else:
+            dkv_acc[:, :, :HD] += d_key
+            dkv_acc[:, :, HD:] += d_value
+
+    pair_dkv = send(dkv_acc.at[other], dkv_pair, pair_s.at[0], pair_r.at[0], pair_dev)
+
+    for copy in at_copies:
+        copy.wait_recv()
+    attention = att_own[...]
+    part = dot_rows(attention, dy_ref[...]).reshape(F, H, 2, -1, dy_ref.shape[1])
+    for j in range(2):
+        go0[j] = part[:, :, j].astype(bf)
+    pair_go = send(go0.at[other], go0_got, pair_s.at[1], pair_r.at[1], pair_dev)
+
+    pair_dkv.wait_recv()
+    dkv = (dkv_acc[c] + dkv_pair[...]).astype(bf)
+    for h in range(H):
+        dkv_send[h] = dkv[h * rows:(h + 1) * rows]
+        d_head[h * rows:(h + 1) * rows, :HD] = dq_send[h]
+    d_head[:, HD:] = dkv
+    dk_copies = []
+    for k in range(1, H):
+        to = lax.rem(z + k, H)
+        dk_copies.append(send(
+            dkv_send.at[to], dkv_own.at[z], dk_s.at[k - 1], dk_r.at[k - 1], head_dev(k)
+        ))
+    dkv_own[z] = dkv_send[z]
+
+    part = dot_rows(xg[c].reshape(H * rows, -1), d_head[...]).reshape(F, H, 2, -1, 3 * HD)
+    for j in range(2):
+        gw0[j] = part[:, :, j].astype(bf)
+    pair_gw = send(gw0.at[other], gw0_got, pair_s.at[2], pair_r.at[2], pair_dev)
+
+    def over_clips(kept, got, out, slots, s, r):
+        out[...] = (kept[c].astype(f32) + got[...].astype(f32)).astype(bf)
+        return [
+            send(out.at[lax.rem(f + k, F)], slots.at[k - 1], s.at[k - 1], r.at[k - 1], clip_dev(k))
+            for k in range(1, F)
+        ]
+
+    def summed(copies, out, slots):
+        total = out[f].astype(f32)
+        for k in range(1, F):
+            copies[k - 1].wait_recv()
+            total = total + slots[k - 1].astype(f32)
+        return total.astype(bf)
+
+    pair_go.wait_recv()
+    go_copies = over_clips(go0, go0_got, go1, go1_got, go1_s, go1_r)
+    mixed_ref[...] = (x_ref[...].astype(f32) + dot_plain(attention, wo_all[...])).astype(bf)
+    pair_gw.wait_recv()
+    gw_copies = over_clips(gw0, gw0_got, gw1, gw1_got, gw1_s, gw1_r)
+
+    for copy in dq_copies:
+        copy.wait_recv()
+    token = dy_ref[...].astype(f32) + contract_cols(dq_own[...], wq_all[...])
+    for copy in dk_copies:
+        copy.wait_recv()
+    dk_rows = jnp.concatenate([dkv_own[h][:, :HD] for h in range(H)], axis=1)
+    dv_rows = jnp.concatenate([dkv_own[h][:, HD:] for h in range(H)], axis=1)
+    token = token + contract_cols(dk_rows, wk_all[...]) + contract_cols(dv_rows, wv_all[...])
+    token_ref[...] = token.astype(bf)
+
+    go2[...] = summed(go_copies, go1, go1_got)
+    go_last = [
+        send(go2.at[lax.rem(z + k, H)], go2_got.at[k - 1], go2_s.at[k - 1], go2_r.at[k - 1], head_dev(k))
+        for k in range(1, H)
+    ]
+    gw2[...] = summed(gw_copies, gw1, gw1_got)
+    gw_last = [
+        send(gw2.at[lax.rem(z + k, H)], gw2_got.at[z], gw2_s.at[k - 1], gw2_r.at[k - 1], head_dev(k))
+        for k in range(1, H)
+    ]
+    gw2_got[z] = gw2[z]
+    total = go2[z].astype(f32)
+    for k in range(1, H):
+        go_last[k - 1].wait_recv()
+        total = total + go2_got[k - 1].astype(f32)
+    go_ref[...] = total
+    for copy in gw_last:
+        copy.wait_recv()
+    for h in range(H):
+        piece = gw2_got[h].astype(f32)
+        gq_ref[:, h * HD:(h + 1) * HD] = piece[:, :HD]
+        gk_ref[:, h * HD:(h + 1) * HD] = piece[:, HD:2 * HD]
+        gv_ref[:, h * HD:(h + 1) * HD] = piece[:, 2 * HD:]
+    for copy in started:
+        copy.wait_send()
+
+
+def fused_body(F, tokens, cotangent, w_query, w_key, w_value, w_out, block_mask, span_order):
+    H = HEADS
+    bf, f32 = jnp.bfloat16, jnp.float32
+    x_rows, dy_rows = tokens[0], cotangent[0]
+    rows, D = x_rows.shape
+    HQ = w_query.shape[1]
+    spans = rows // SPAN
+    n_spans = span_order.shape[0]
+    per_block = BLK // SPAN
+    order = span_order.reshape(H, 2, spans).transpose(1, 0, 2).reshape(-1) // per_block
+    hot = (order[:, None] == jnp.arange(block_mask.shape[0])[None, :]).astype(f32)
+    linked = jnp.dot(jnp.dot(hot, (block_mask == 1).astype(f32)), hot.T)
+    bias = jnp.where(linked > 0.5, 0.0, NEG).astype(f32)
+    bias = jnp.broadcast_to(bias[:, :, None], (n_spans, n_spans, SPAN))
+    bias = bias.reshape(2, H, spans, n_spans * SPAN)
+
+    gq_rows = D // (F * H * 2)
+    go_rows = HQ // (F * H * 2)
+    V = pltpu.VMEM
+    dma = pltpu.SemaphoreType.DMA
+    hr = H * rows
+    scratch = [
+        V((2, H, rows, D), bf), V((D, HQ), bf), V((D, HQ), bf), V((D, HQ), bf), V((HQ, D), bf),
+        V((D, 3 * HD), bf), V((H, rows, HD), bf), V((H, rows, HD), bf),
+        V((2, hr, 2 * HD), bf), V((H, rows, HD), bf),
+        V((H, rows, HD), bf), V((rows, HQ), bf), V((H, rows, HD), bf), V((rows, HQ), bf),
+        V((2, hr, 2 * HD), f32), V((hr, 2 * HD), f32), V((H, rows, 2 * HD), bf),
+        V((H, rows, 2 * HD), bf), V((hr, 3 * HD), bf),
+        V((2, F, H, go_rows, D), bf), V((F, H, go_rows, D), bf), V((F, H, go_rows, D), bf),
+        V((F - 1, H, go_rows, D), bf), V((H, go_rows, D), bf), V((H - 1, go_rows, D), bf),
+        V((2, F, H, gq_rows, 3 * HD), bf), V((F, H, gq_rows, 3 * HD), bf),
+        V((F, H, gq_rows, 3 * HD), bf), V((F - 1, H, gq_rows, 3 * HD), bf),
+        V((H, gq_rows, 3 * HD), bf), V((H, gq_rows, 3 * HD), bf),
+    ]
+    for shape in (
+        (H - 1,), (H,), (4, F - 1), (4, F - 1), (H - 1,), (H - 1,), (H - 1,), (H - 1,), (3,),
+        (F - 1,), (H - 1,), (F - 1,), (H - 1,),
+    ):
+        scratch += [dma(shape), dma(shape)]
+    mixed, token, gq, gk, gv, go = pl.pallas_call(
+        functools.partial(fused_kernel, F),
+        out_shape=(
+            jax.ShapeDtypeStruct((rows, D), bf), jax.ShapeDtypeStruct((rows, D), bf),
+            jax.ShapeDtypeStruct((gq_rows, HQ), f32), jax.ShapeDtypeStruct((gq_rows, HQ), f32),
+            jax.ShapeDtypeStruct((gq_rows, HQ), f32), jax.ShapeDtypeStruct((go_rows, D), f32),
+        ),
+        in_specs=[pl.BlockSpec(memory_space=pltpu.VMEM)] * 7,
+        out_specs=tuple([pl.BlockSpec(memory_space=pltpu.VMEM)] * 6),
+        scratch_shapes=scratch,
+        compiler_params=pltpu.CompilerParams(
+            collective_id=0, has_side_effects=True, vmem_limit_bytes=48 * 1024 * 1024
+        ),
+        cost_estimate=pl.CostEstimate(
+            flops=3 * 10**9, bytes_accessed=4 * 10**6, transcendentals=10**6
+        ),
+    )(x_rows, dy_rows, w_query, w_key, w_value, w_out, bias)
+    return (mixed[None], token[None], gq, gk, gv, go)
+
+
 def solution(mesh):
+    shape = dict(mesh.shape)
+    chosen = body
+    if shape["ctx"] == 2 * HEADS and shape["fsdp"] == 4:
+        chosen = functools.partial(fused_body, shape["fsdp"])
     return jax.shard_map(
-        body,
+        chosen,
         mesh=mesh,
         in_specs=(
             P("fsdp", "ctx", None),

time: 788 us -> 72.1 us (0.09)
  waiting for transfers between devices: 683 us -> 0 us
  Pallas kernels: 0 us -> 60.4 us
  matrix products: 35.1 us -> 0.99 us
  blocking collectives: 25.7 us -> 0 us
  between operations: 14.5 us -> 0.69 us
  local copies, waits for them, and re-layouts: 22.8 us -> 9.75 us
    unnamed x15 -> x0, waiting for transfers between devices: 398 us -> none
    all_gather x8 -> x0, waiting for transfers between devices: 149 us -> none  [the longest x1 29.2 us: body(): lax.all_gather(w_key, 'fsdp', axis=0, tiled=True)]
    reduce_scatter x1 -> x0, waiting for transfers between devices: 137 us -> none  [body(): lax.psum_scatter(grad_o, ('fsdp', 'ctx'), scatter_dimension=0, tiled=True)]
    pallas_call x0 -> x1, Pallas kernels: none -> 60.4 us  [fused_body(): pl.pallas_call(functools.partial(fused_kernel, F), out_shape=(jax.ShapeDt...]
    dot_general x34 -> x1, matrix products: 35.1 us -> 0.99 us  [fused_body(): linked = jnp.dot(jnp.dot(hot, (block_mask == 1).astype(f32)), hot.T)]
    all_gather x2 -> x0, blocking collectives: 25.7 us -> none  [the longest x1 13 us: body(): lax.all_gather(log_rows, 'ctx', axis=0, tiled=True)]
    dynamic_slice x16 -> x0, local copies, waits for them, and re-layouts: 9.3 us -> none  [over_blocks(): carry, _ = lax.scan(scan_step, carry, (numbers, stacked))]
  transfers between devices with their start and end apart: 12 -> 0, of which waited for: 10 -> 0; matrix products, arithmetic and copies ran while one was open for 5% -> 0% of each run, Pallas kernels for 0% -> 0%
where the time goes in v1:
time: 72.1 us; the launch traced here: 71.8 us
  Pallas kernels  60.4 us (84%)
  local copies, waits for them, and re-layouts  9.75 us (14%)
  matrix products  0.99 us (1%)
    pallas_call x1, Pallas kernels, fused_body(): pl.pallas_call(functools.partial(fused_kernel, F), out_shape=(jax.ShapeDt...  60.4 us
    unnamed x18, local copies, waits for them, and re-layouts  8.67 us

profile of v1, /device:TPU:0, one launch (start us, length us, event | category | flops | bytes accessed | tf_op | source)
XLA Modules:
  0.0 71.8 jit_solution(3028003277587818418)
XLA Ops:
  0.6 0.0 copy-start
  0.6 0.8 %reshape.50 = s32[4,2,2]{2,1,0:T(2,128)S(1)} reshape(s32[16]{0:T(128)} %param.15) | data formatting | bytes 128 | tf_op jit(solution)/shard_map/reshape | solution.py:477
  1.4 0.1 reshape.51
  1.5 1.0 %fusion.6 = f32[16,16]{1,0:T(8,128)S(1)} fusion(s32[16]{0:T(128)S(1)} %and_select_fusion, s32[8,8]{1,0:T(8,128)} %param.14), kind=kOutput, calls=%fused_computation.3 | convolution fusion | flops 6976 | bytes 1344 | tf_op jit(solution)/shard_map/dot_general | solution.py:479
  2.5 0.1 broadcast_in_dim.24
  2.6 0.1 reshape.52.bias_ref
  2.7 0.0 copy-done
  2.8 0.0 copy-start.1
  2.8 0.9 %copy-done.1 = bf16[1,128,1024]{2,1,0:T(8,128)(2,1)S(1)} copy-done((bf16[1,128,1024]{2,1,0:T(8,128)(2,1)S(1)}, bf16[1,128,1024]{2,1,0:T(8,128)(2,1)}, u32[]{:S(2)}) %copy-start.1) | copy-done | bytes 262168
  3.7 0.0 copy-start.2
  3.7 0.9 %copy-done.2 = bf16[256,512]{1,0:T(8,128)(2,1)S(1)} copy-done((bf16[256,512]{1,0:T(8,128)(2,1)S(1)}, bf16[256,512]{1,0:T(8,128)(2,1)}, u32[]{:S(2)}) %copy-start.2) | copy-done | bytes 262168
  4.7 0.0 copy-start.3
  4.7 0.9 %copy-done.3 = bf16[256,512]{1,0:T(8,128)(2,1)S(1)} copy-done((bf16[256,512]{1,0:T(8,128)(2,1)S(1)}, bf16[256,512]{1,0:T(8,128)(2,1)}, u32[]{:S(2)}) %copy-start.3) | copy-done | bytes 262168
  5.6 0.0 copy-start.4
  5.6 0.9 %copy-done.4 = bf16[256,512]{1,0:T(8,128)(2,1)S(1)} copy-done((bf16[256,512]{1,0:T(8,128)(2,1)S(1)}, bf16[256,512]{1,0:T(8,128)(2,1)}, u32[]{:S(2)}) %copy-start.4) | copy-done | bytes 262168
  6.6 0.0 copy-start.5
  6.6 0.9 %copy-done.5 = bf16[128,1024]{1,0:T(8,128)(2,1)S(1)} copy-done((bf16[128,1024]{1,0:T(8,128)(2,1)S(1)}, bf16[128,1024]{1,0:T(8,128)(2,1)}, u32[]{:S(2)}) %copy-start.5) | copy-done | bytes 262168
  7.5 60.4 %shard_map.127 = (bf16[128,1024]{1,0:T(8,128)(2,1)S(1)}, bf16[128,1024]{1,0:T(8,128)(2,1)S(1)}, f32[32,512]{1,0:T(8,128)S(1)}, f32[32,512]{1,0:T(8,128)S(1)}, f3...) custom-call(bf16[128,1024]{1,0:T(8,128)(2,1)S(1)} %bitcast.7, bf16[128,1024]{1,0:T(8,128)(2,1)S(1)} %bitcast.8, ...), custom_call_target="tpu_custom_call" | custom-call | flops 3000000000 | bytes 4000000 | tf_op jit(solution)/shard_map/pallas_call | solution.py:507
  67.9 0.7 copy.22
  68.6 0.7 copy.23
  69.3 0.6 copy.24
  69.9 0.6 copy.25
  70.5 0.6 copy.26
  71.2 0.6 copy.27
  (2 shorter events, 0.0 us)
Async XLA Ops:
  0.6 2.1 %copy-start = (bf16[1,128,1024]{2,1,0:T(8,128)(2,1)S(1)}, bf16[1,128,1024]{2,1,0:T(8,128)(2,1)}, u32[]{:S(2)}) copy-start(bf16[1,128,1024]{2,1,0:T(8,128)(2,1)} %param.8) | copy-start | bytes 786436
  2.8 1.0 %copy-start.1 = (bf16[1,128,1024]{2,1,0:T(8,128)(2,1)S(1)}, bf16[1,128,1024]{2,1,0:T(8,128)(2,1)}, u32[]{:S(2)}) copy-start(bf16[1,128,1024]{2,1,0:T(8,128)(2,1)} %param.9) | copy-start | bytes 786436
  3.7 0.9 %copy-start.2 = (bf16[256,512]{1,0:T(8,128)(2,1)S(1)}, bf16[256,512]{1,0:T(8,128)(2,1)}, u32[]{:S(2)}) copy-start(bf16[256,512]{1,0:T(8,128)(2,1)} %wq_ref.1) | copy-start | bytes 786436
  4.7 0.9 %copy-start.3 = (bf16[256,512]{1,0:T(8,128)(2,1)S(1)}, bf16[256,512]{1,0:T(8,128)(2,1)}, u32[]{:S(2)}) copy-start(bf16[256,512]{1,0:T(8,128)(2,1)} %wk_ref.1) | copy-start | bytes 786436
  5.6 0.9 %copy-start.4 = (bf16[256,512]{1,0:T(8,128)(2,1)S(1)}, bf16[256,512]{1,0:T(8,128)(2,1)}, u32[]{:S(2)}) copy-start(bf16[256,512]{1,0:T(8,128)(2,1)} %wv_ref.1) | copy-start | bytes 786436
  6.6 0.9 %copy-start.5 = (bf16[128,1024]{1,0:T(8,128)(2,1)S(1)}, bf16[128,1024]{1,0:T(8,128)(2,1)}, u32[]{:S(2)}) copy-start(bf16[128,1024]{1,0:T(8,128)(2,1)} %wo_ref.1) | copy-start | bytes 786436

commit v2 on v1

--- a/solution.py
+++ b/solution.py
@@ -210,13 +210,14 @@
 
 def fused_kernel(
     F,
-    x_ref, dy_ref, wq_ref, wk_ref, wv_ref, wo_ref, bias_ref,
+    x_ref, dy_ref, wq_ref, wk_ref, wv_ref, wo_ref, mask_ref, order_ref,
     mixed_ref, token_ref, gq_ref, gk_ref, gv_ref, go_ref,
-    xg, wq_all, wk_all, wv_all, wo_all, wh, g_send, g_got, kv_buf, q_buf,
+    xg, dy_own, wq_all, wk_all, wv_all, wo_all, wh, bias, g_send, g_got, kv_buf, q_buf,
     att_send, att_own, dq_send, dq_own, dkv_acc, dkv_pair, dkv_send, dkv_own, d_head,
     go0, go0_got, go1, go1_got, go2, go2_got,
     gw0, gw0_got, gw1, gw1_got, gw2, gw2_got,
-    x_s, x_r, xf_s, xf_r, w_s, w_r, wf_s, wf_r, g_s, g_r, at_s, at_r, dq_s, dq_r,
+    here, x_s, x_r, xf_s, xf_r, w_s, w_r, wf_s, wf_r, wh_s, wh_r, whf_s, whf_r,
+    own_s, own_r, g_s, g_r, at_s, at_r, dq_s, dq_r,
     dk_s, dk_r, pair_s, pair_r, go1_s, go1_r, go2_s, go2_r, gw1_s, gw1_r, gw2_s, gw2_r,
 ):
     H = HEADS
@@ -240,14 +241,42 @@
 
     started = []
 
-    def send(src, dst, s, r, dev):
-        copy = pltpu.make_async_remote_copy(
+    def remote(src, dst, s, r, dev):
+        return pltpu.make_async_remote_copy(
             src_ref=src, dst_ref=dst, send_sem=s, recv_sem=r,
             device_id=dev, device_id_type=pl.DeviceIdType.MESH,
         )
+
+    def send(src, dst, s, r, dev):
+        copy = remote(src, dst, s, r, dev)
         copy.start()
         started.append(copy)
         return copy
+
+    cols = pl.ds(pl.multiple_of(z * HD, HD), HD)
+    weights = ((wo_ref, wo_all), (wk_ref, wk_all), (wv_ref, wv_all), (wq_ref, wq_all))
+    heads = ((wk_ref, 0), (wv_ref, 1), (wq_ref, 2))
+
+    def shard(i, owner):
+        n = weights[i][0].shape[0]
+        return weights[i][1].at[pl.ds(pl.multiple_of(owner * n, n), n)]
+
+    shard_rows = wk_ref.shape[0]
+    half_rows = shard_rows // 2
+
+    def head_rows(i, owner, part):
+        start = pl.multiple_of(owner * shard_rows + part * half_rows, half_rows)
+        return wh.at[pl.ds(start, half_rows), pl.ds(i * HD, HD)]
+
+    moves = [(x_ref, xg.at[c, z]), (dy_ref, dy_own)]
+    moves += [(weights[i][0], shard(i, f)) for i in range(4)]
+    moves += [
+        (ref.at[:, cols], wh.at[pl.ds(pl.multiple_of(f * shard_rows, shard_rows), shard_rows), pl.ds(i * HD, HD)])
+        for ref, i in heads
+    ]
+    local = [pltpu.make_async_copy(a, b, here.at[n]) for n, (a, b) in enumerate(moves)]
+    for copy in local:
+        copy.start()
 
     barrier = pltpu.get_barrier_semaphore()
     peers = [pair_dev] + [head_dev(k) for k in range(1, H)] + [clip_dev(k) for k in range(1, F)]
@@ -255,7 +284,34 @@
         pl.semaphore_signal(barrier, inc=1, device_id=dev, device_id_type=pl.DeviceIdType.MESH)
     pl.semaphore_wait(barrier, len(peers))
 
-    weights = ((wo_ref, wo_all), (wk_ref, wk_all), (wv_ref, wv_all), (wq_ref, wq_all))
+    def flow(side, s):
+        step = 1 if side == 0 else -1
+        sent = z - step * s
+        got = z - step * (s + 1)
+        inside = (sent >= 0) & (sent <= H - 1)
+        can_send = inside & (z < H - 1 if side == 0 else z > 0)
+        can_recv = (got >= 0) & (got <= H - 1)
+        src = x_ref if s == 0 else xg.at[c, sent]
+        out = remote(src, xg.at[c, sent], x_s.at[side, s], x_r.at[side, s], (f, (z + step) * 2 + c))
+        into = remote(src, xg.at[c, got], x_s.at[side, s], x_r.at[side, s], (f, (z + step) * 2 + c))
+        part = xg.at[c, got]
+        pair = remote(part, part, xf_s.at[side, s], xf_r.at[side, s], pair_dev)
+        return can_send, can_recv, out, into, pair, got
+
+    flows = {(side, s): flow(side, s) for s in range(H - 1) for side in range(2)}
+
+    for side in range(2):
+        can_send, _, out, _, _, _ = flows[side, 0]
+        pl.when(can_send)(out.start)
+    x_own = send(x_ref, xg.at[c, z], own_s.at[0], own_r.at[0], pair_dev)
+
+    wh_copies = {}
+    for ref, i in heads:
+        src = ref.at[pl.ds(pl.multiple_of(c * half_rows, half_rows), half_rows), cols]
+        for k in range(1, F):
+            wh_copies[i, k] = send(
+                src, head_rows(i, f, c), wh_s.at[i, k - 1], wh_r.at[i, k - 1], clip_dev(k)
+            )
 
     def half_of(i, owner, part):
         n = weights[i][0].shape[0]
@@ -271,18 +327,7 @@
             for k in range(1, F)
         ]
 
-    w_copies = [w_send(0)]
-    x_copies = [
-        send(x_ref, xg.at[c, z], x_s.at[k - 1], x_r.at[k - 1], head_dev(k)) for k in range(1, H)
-    ]
-    x_pair = [send(x_ref, xg.at[c, z], xf_s.at[0], xf_r.at[0], pair_dev)]
-    for i in range(1, 4):
-        w_copies.append(w_send(i))
-
-    xg[c, z] = x_ref[...]
-    for ref, whole in weights:
-        n = ref.shape[0]
-        whole[pl.ds(pl.multiple_of(f * n, n), n), :] = ref[...]
+    w_copies = {0: w_send(0)}
 
     def w_forward(i):
         out = []
@@ -292,16 +337,77 @@
             out.append(send(part, part, wf_s.at[i, k - 1], wf_r.at[i, k - 1], pair_dev))
         return out
 
-    def x_forward(k):
-        x_copies[k - 1].wait_recv()
-        part = xg.at[c, lax.rem(z + H - k, H)]
-        x_pair.append(send(part, part, xf_s.at[k], xf_r.at[k], pair_dev))
-
-    for copy in w_forward(0):
-        copy.wait_recv()
-    g_all = lax.dot_general(
-        dy_ref[...], wo_all[...], (((1,), (1,)), ((), ())), preferred_element_type=f32
-    ).astype(bf)
+    spans = rows // SPAN
+    per_block = BLK // SPAN
+    width = bias.shape[1]
+    place = lax.broadcasted_iota(jnp.int32, (1, width), 1) // SPAN
+    key_block = [
+        order_ref[(2 * h + j) * spans + s] // per_block
+        for j in range(2) for h in range(H) for s in range(spans)
+    ]
+    for h in range(H):
+        for s in range(spans):
+            block = order_ref[(2 * h + c) * spans + s] // per_block
+            line = jnp.full((1, width), NEG, f32)
+            for n, key in enumerate(key_block):
+                open_to = jnp.where(mask_ref[block, key] == 1, 0.0, NEG).astype(f32)
+                line = jnp.where(place == n, open_to, line)
+            bias[h * spans + s:h * spans + s + 1, :] = line
+
+    for copy in local:
+        copy.wait()
+
+    forwards = []
+    for k in range(1, F):
+        for _, i in heads:
+            wh_copies[i, k].wait_recv()
+            part = head_rows(i, lax.rem(f + F - k, F), c)
+            forwards.append(send(part, part, whf_s.at[i, k - 1], whf_r.at[i, k - 1], pair_dev))
+
+    def pass_on(s):
+        for side in range(2):
+            _, can_recv, _, into, pair, _ = flows[side, s]
+
+            @pl.when(can_recv)
+            def _():
+                into.wait_recv()
+                pair.start()
+
+            if s < H - 2:
+                can_send, _, out, _, _, _ = flows[side, s + 1]
+                pl.when(can_send)(out.start)
+
+    def project_own(slot):
+        out = dot_plain(xg[c, slot], wh[...]).astype(bf)
+        kv_buf[c, slot] = out[:, :2 * HD]
+        q_buf[slot] = out[:, 2 * HD:]
+
+    def project_pair(slot):
+        kv_buf[other, slot] = dot_plain(xg[other, slot], wh[:, :2 * HD]).astype(bf)
+
+    def project(s):
+        for side in range(2):
+            _, can_recv, _, _, pair, got = flows[side, s]
+
+            @pl.when(can_recv)
+            def _():
+                project_own(got)
+                pair.wait_recv()
+                project_pair(got)
+
+    pass_on(0)
+    wo_forwards = w_forward(0)
+    for i in range(1, 4):
+        w_copies[i] = w_send(i)
+    for copy in forwards:
+        copy.wait_recv()
+    project_own(z)
+    x_own.wait_recv()
+    project_pair(z)
+    pass_on(1)
+    for copy in wo_forwards:
+        copy.wait_recv()
+    g_all = contract_cols(dy_own[...], wo_all[...]).astype(bf)
     for h in range(H):
         g_send[h] = g_all[:, h * HD:(h + 1) * HD]
     g_copies = []
@@ -309,44 +415,29 @@
         to = lax.rem(z + k, H)
         g_copies.append(send(g_send.at[to], g_got.at[z], g_s.at[k - 1], g_r.at[k - 1], head_dev(k)))
     g_got[z] = g_send[z]
-
-    forwards = []
-    forwards += w_forward(1)
-    x_forward(1)
-    forwards += w_forward(2)
-    x_forward(3)
-    x_forward(2)
-    forwards += w_forward(3)
-    for copy in forwards:
-        copy.wait_recv()
-    cols = pl.ds(pl.multiple_of(z * HD, HD), HD)
-    wh[:, :HD] = wk_all[:, cols]
-    wh[:, HD:2 * HD] = wv_all[:, cols]
-    wh[:, 2 * HD:] = wq_all[:, cols]
-    own_x = xg[c].reshape(H * rows, -1)
-    own_kvq = dot_plain(own_x, wh[...]).astype(bf)
-    kv_buf[c] = own_kvq[:, :2 * HD]
-    for h in range(H):
-        q_buf[h] = own_kvq[h * rows:(h + 1) * rows, 2 * HD:]
-    for copy in x_pair:
-        copy.wait_recv()
-    kv_buf[other] = dot_plain(xg[other].reshape(H * rows, -1), wh[:, :2 * HD]).astype(bf)
+    project(0)
+    project(1)
+    pass_on(2)
+    project(2)
     for copy in g_copies:
         copy.wait_recv()
 
     kv = kv_buf[...].reshape(2 * H * rows, 2 * HD)
     keys = kv[:, :HD]
     values = kv[:, HD:]
-    spans = rows // SPAN
     at_copies, dq_copies = [], []
+    late = []
     for k in (1, 2, 3, 0):
         h = lax.rem(z + k, H)
         query = q_buf[h]
         grad = g_got[h]
         score = contract_cols(query, keys) * scale
-        line = bias_ref[c, h]
         score = score + jnp.concatenate(
-            [jnp.broadcast_to(line[s:s + 1], (SPAN, line.shape[1])) for s in range(spans)], axis=0
+            [
+                jnp.broadcast_to(bias[pl.ds(h * spans + s, 1), :], (SPAN, width))
+                for s in range(spans)
+            ],
+            axis=0,
         )
         prob = jnp.exp(score - jnp.max(score, axis=1, keepdims=True))
         prob = prob * (1.0 / jnp.sum(prob, axis=1, keepdims=True))
@@ -379,12 +470,14 @@
             dkv_acc[:, :, :HD] += d_key
             dkv_acc[:, :, HD:] += d_value
 
+    for i in (3, 1, 2):
+        late += w_forward(i)
     pair_dkv = send(dkv_acc.at[other], dkv_pair, pair_s.at[0], pair_r.at[0], pair_dev)
 
     for copy in at_copies:
         copy.wait_recv()
     attention = att_own[...]
-    part = dot_rows(attention, dy_ref[...]).reshape(F, H, 2, -1, dy_ref.shape[1])
+    part = dot_rows(attention, dy_own[...]).reshape(F, H, 2, -1, dy_own.shape[1])
     for j in range(2):
         go0[j] = part[:, :, j].astype(bf)
     pair_go = send(go0.at[other], go0_got, pair_s.at[1], pair_r.at[1], pair_dev)
@@ -424,13 +517,15 @@
 
     pair_go.wait_recv()
     go_copies = over_clips(go0, go0_got, go1, go1_got, go1_s, go1_r)
-    mixed_ref[...] = (x_ref[...].astype(f32) + dot_plain(attention, wo_all[...])).astype(bf)
+    mixed_ref[...] = (xg[c, z].astype(f32) + dot_plain(attention, wo_all[...])).astype(bf)
     pair_gw.wait_recv()
     gw_copies = over_clips(gw0, gw0_got, gw1, gw1_got, gw1_s, gw1_r)
 
     for copy in dq_copies:
         copy.wait_recv()
-    token = dy_ref[...].astype(f32) + contract_cols(dq_own[...], wq_all[...])
+    for copy in late:
+        copy.wait_recv()
+    token = dy_own[...].astype(f32) + contract_cols(dq_own[...], wq_all[...])
     for copy in dk_copies:
         copy.wait_recv()
     dk_rows = jnp.concatenate([dkv_own[h][:, :HD] for h in range(H)], axis=1)
@@ -463,6 +558,19 @@
         gv_ref[:, h * HD:(h + 1) * HD] = piece[:, 2 * HD:]
     for copy in started:
         copy.wait_send()
+    for can_send, can_recv, out, _, pair, _ in flows.values():
+        pl.when(can_send)(out.wait_send)
+        pl.when(can_recv)(pair.wait_send)
+
+
+def store_kernel(*refs):
+    n = (len(refs) - 1) // 2
+    sems = refs[-1]
+    copies = [pltpu.make_async_copy(refs[i], refs[n + i], sems.at[i]) for i in range(n)]
+    for copy in copies:
+        copy.start()
+    for copy in copies:
+        copy.wait()
 
 
 def fused_body(F, tokens, cotangent, w_query, w_key, w_value, w_out, block_mask, span_order):
@@ -471,25 +579,15 @@
     x_rows, dy_rows = tokens[0], cotangent[0]
     rows, D = x_rows.shape
     HQ = w_query.shape[1]
-    spans = rows // SPAN
-    n_spans = span_order.shape[0]
-    per_block = BLK // SPAN
-    order = span_order.reshape(H, 2, spans).transpose(1, 0, 2).reshape(-1) // per_block
-    hot = (order[:, None] == jnp.arange(block_mask.shape[0])[None, :]).astype(f32)
-    linked = jnp.dot(jnp.dot(hot, (block_mask == 1).astype(f32)), hot.T)
-    bias = jnp.where(linked > 0.5, 0.0, NEG).astype(f32)
-    bias = jnp.broadcast_to(bias[:, :, None], (n_spans, n_spans, SPAN))
-    bias = bias.reshape(2, H, spans, n_spans * SPAN)
-
     gq_rows = D // (F * H * 2)
     go_rows = HQ // (F * H * 2)
     V = pltpu.VMEM
     dma = pltpu.SemaphoreType.DMA
     hr = H * rows
     scratch = [
-        V((2, H, rows, D), bf), V((D, HQ), bf), V((D, HQ), bf), V((D, HQ), bf), V((HQ, D), bf),
-        V((D, 3 * HD), bf), V((H, rows, HD), bf), V((H, rows, HD), bf),
-        V((2, hr, 2 * HD), bf), V((H, rows, HD), bf),
+        V((2, H, rows, D), bf), V((rows, D), bf), V((D, HQ), bf), V((D, HQ), bf), V((D, HQ), bf), V((HQ, D), bf),
+        V((D, 3 * HD), bf), V((hr // SPAN, 2 * hr), f32), V((H, rows, HD), bf), V((H, rows, HD), bf),
+        V((2, H, rows, 2 * HD), bf), V((H, rows, HD), bf),
         V((H, rows, HD), bf), V((rows, HQ), bf), V((H, rows, HD), bf), V((rows, HQ), bf),
         V((2, hr, 2 * HD), f32), V((hr, 2 * HD), f32), V((H, rows, 2 * HD), bf),
         V((H, rows, 2 * HD), bf), V((hr, 3 * HD), bf),
@@ -499,28 +597,39 @@
         V((F, H, gq_rows, 3 * HD), bf), V((F - 1, H, gq_rows, 3 * HD), bf),
         V((H, gq_rows, 3 * HD), bf), V((H, gq_rows, 3 * HD), bf),
     ]
+    scratch.append(dma((9,)))
     for shape in (
-        (H - 1,), (H,), (4, F - 1), (4, F - 1), (H - 1,), (H - 1,), (H - 1,), (H - 1,), (3,),
+        (2, H - 1), (2, H - 1), (4, F - 1), (4, F - 1), (3, F - 1), (3, F - 1), (1,), (H - 1,), (H - 1,), (H - 1,), (H - 1,), (3,),
         (F - 1,), (H - 1,), (F - 1,), (H - 1,),
     ):
         scratch += [dma(shape), dma(shape)]
-    mixed, token, gq, gk, gv, go = pl.pallas_call(
+    vmem = pl.BlockSpec(memory_space=pltpu.VMEM)
+    smem = pl.BlockSpec(memory_space=pltpu.SMEM)
+    results = pl.pallas_call(
         functools.partial(fused_kernel, F),
         out_shape=(
             jax.ShapeDtypeStruct((rows, D), bf), jax.ShapeDtypeStruct((rows, D), bf),
             jax.ShapeDtypeStruct((gq_rows, HQ), f32), jax.ShapeDtypeStruct((gq_rows, HQ), f32),
             jax.ShapeDtypeStruct((gq_rows, HQ), f32), jax.ShapeDtypeStruct((go_rows, D), f32),
         ),
-        in_specs=[pl.BlockSpec(memory_space=pltpu.VMEM)] * 7,
-        out_specs=tuple([pl.BlockSpec(memory_space=pltpu.VMEM)] * 6),
+        in_specs=[pl.BlockSpec(memory_space=pltpu.HBM)] * 6 + [smem] * 2,
+        out_specs=tuple([vmem] * 6),
         scratch_shapes=scratch,
         compiler_params=pltpu.CompilerParams(
-            collective_id=0, has_side_effects=True, vmem_limit_bytes=48 * 1024 * 1024
+            collective_id=0, has_side_effects=True, vmem_limit_bytes=60 * 1024 * 1024
         ),
         cost_estimate=pl.CostEstimate(
             flops=3 * 10**9, bytes_accessed=4 * 10**6, transcendentals=10**6
         ),
-    )(x_rows, dy_rows, w_query, w_key, w_value, w_out, bias)
+    )(x_rows, dy_rows, w_query, w_key, w_value, w_out, block_mask, span_order)
+    mixed, token, gq, gk, gv, go = pl.pallas_call(
+        store_kernel,
+        out_shape=tuple(jax.ShapeDtypeStruct(r.shape, r.dtype) for r in results),
+        in_specs=[pl.BlockSpec(memory_space=pltpu.HBM)] * 6,
+        out_specs=tuple([pl.BlockSpec(memory_space=pltpu.HBM)] * 6),
+        scratch_shapes=[dma((6,))],
+        compiler_params=pltpu.CompilerParams(vmem_limit_bytes=60 * 1024 * 1024),
+    )(*results)
     return (mixed[None], token[None], gq, gk, gv, go)
 
 

time: 72.1 us -> 84.1 us (1.17)
  Pallas kernels: 60.4 us -> 83.3 us
  local copies, waits for them, and re-layouts: 9.75 us -> 0 us
  matrix products: 0.99 us -> 0 us
    pallas_call x0 -> x1, Pallas kernels: none -> 25 us  [fused_body(): pl.pallas_call(store_kernel, out_shape=tuple((jax.ShapeDtypeStruct(r.shap...]
    unnamed x18 -> x0, local copies, waits for them, and re-layouts: 8.67 us -> none
    pallas_call x1, Pallas kernels: 60.4 us -> 58.3 us  [fused_body(): pl.pallas_call(functools.partial(fused_kernel, F), out_shape=(jax.ShapeDt...]
    dot_general x1 -> x0, matrix products: 0.99 us -> none  [fused_body(): linked = jnp.dot(jnp.dot(hot, (block_mask == 1).astype(f32)), hot.T)]
    reshape x3 -> x0, local copies, waits for them, and re-layouts: 0.98 us -> none  [the longest x2 0.87 us: fused_body(): span_order.reshape(H, 2, spans).transpose(1, 0, 2).reshape(-1) // per_block]
where the time goes in v2:
time: 84.1 us; the launch traced here: 83.9 us
  Pallas kernels  83.3 us (99%)
    pallas_call x1, Pallas kernels, fused_body(): pl.pallas_call(functools.partial(fused_kernel, F), out_shape=(jax.ShapeDt...  58.3 us
    pallas_call x1, Pallas kernels, fused_body(): pl.pallas_call(store_kernel, out_shape=tuple((jax.ShapeDtypeStruct(r.shap...  25 us

profile of v2, /device:TPU:0, one launch (start us, length us, event | category | flops | bytes accessed | tf_op | source)
XLA Modules:
  0.0 83.9 jit_solution(11868988643862179839)
XLA Ops:
  0.6 58.3 %shard_map.127 = (bf16[128,1024]{1,0:T(8,128)(2,1)}, bf16[128,1024]{1,0:T(8,128)(2,1)}, f32[32,512]{1,0:T(8,128)}, f32[32,512]{1,0:T(8,128)}, f32[32,512]{1,0:T(8,128)}, /*index=5*/f32[16,1024]{1,0:T(8,128)}) custom-call(bf16[128,1024]{1,0:T(8,128)(2,1)} %bitcast.4, bf16[128,1024]{1,0:T(8,128)(2,1)} %bitcast.5, bf16[256,512]{1,0:T(8,128)(2,1)} %wq_ref.1, ...), custom_call_target="tpu_custom_call" | custom-call | flops 3000000000 | bytes 4000000 | tf_op jit(solution)/shard_map/pallas_call | solution.py:608
  58.9 25.0 %shard_map.128 = (bf16[128,1024]{1,0:T(8,128)(2,1)}, bf16[128,1024]{1,0:T(8,128)(2,1)}, f32[32,512]{1,0:T(8,128)}, f32[32,512]{1,0:T(8,128)}, f32[32,512]{1,0:T(8,128)}, /*index=5*/f32[16,1024]{1,0:T(8,128)}) custom-call(bf16[128,1024]{1,0:T(8,128)(2,1)} %get-tuple-element.18.refs_0_, bf16[128,1024]{1,0:T(8,128)(2,1)} %get-tuple-element.19.refs_1_, ...), custom_call_target="tpu_custom_call" | custom-call | tf_op jit(solution)/shard_map/pallas_call | solution.py:625

commit v3 on v2

--- a/solution.py
+++ b/solution.py
@@ -213,12 +213,15 @@
     x_ref, dy_ref, wq_ref, wk_ref, wv_ref, wo_ref, mask_ref, order_ref,
     mixed_ref, token_ref, gq_ref, gk_ref, gv_ref, go_ref,
     xg, dy_own, wq_all, wk_all, wv_all, wo_all, wh, bias, g_send, g_got, kv_buf, q_buf,
-    att_send, att_own, dq_send, dq_own, dkv_acc, dkv_pair, dkv_send, dkv_own, d_head,
+    att_send, att_own, dq_send, dq_own, dk_send, dk_own, dv_send, dv_own,
+    p_buf, dk_acc, dk_pair, dv_acc, dv_pair, xt,
     go0, go0_got, go1, go1_got, go2, go2_got,
+    gv0, gv0_got, gv1, gv1_got, gv2, gv2_got,
     gw0, gw0_got, gw1, gw1_got, gw2, gw2_got,
     here, x_s, x_r, xf_s, xf_r, w_s, w_r, wf_s, wf_r, wh_s, wh_r, whf_s, whf_r,
     own_s, own_r, g_s, g_r, at_s, at_r, dq_s, dq_r,
-    dk_s, dk_r, pair_s, pair_r, go1_s, go1_r, go2_s, go2_r, gw1_s, gw1_r, gw2_s, gw2_r,
+    dk_s, dk_r, dv_s, dv_r, pair_s, pair_r, go1_s, go1_r, go2_s, go2_r,
+    gv1_s, gv1_r, gv2_s, gv2_r, gw1_s, gw1_r, gw2_s, gw2_r,
 ):
     H = HEADS
     f = lax.axis_index("fsdp")
@@ -381,6 +384,7 @@
         out = dot_plain(xg[c, slot], wh[...]).astype(bf)
         kv_buf[c, slot] = out[:, :2 * HD]
         q_buf[slot] = out[:, 2 * HD:]
+        xt[:, pl.ds(pl.multiple_of(slot * rows, rows), rows)] = xg[c, slot].T
 
     def project_pair(slot):
         kv_buf[other, slot] = dot_plain(xg[other, slot], wh[:, :2 * HD]).astype(bf)
@@ -425,81 +429,79 @@
     kv = kv_buf[...].reshape(2 * H * rows, 2 * HD)
     keys = kv[:, :HD]
     values = kv[:, HD:]
-    at_copies, dq_copies = [], []
-    late = []
-    for k in (1, 2, 3, 0):
-        h = lax.rem(z + k, H)
-        query = q_buf[h]
-        grad = g_got[h]
-        score = contract_cols(query, keys) * scale
+    blocks = ((1, 2), (3, 0))
+
+    def slots_of(ks):
+        return [lax.rem(z + k, H) for k in ks]
+
+    def stacked(buf, ks):
+        return jnp.concatenate([buf[h] for h in slots_of(ks)], axis=0)
+
+    def deal(value, ks, slots, own, s, r):
+        out = []
+        for n, (k, h) in enumerate(zip(ks, slots_of(ks))):
+            piece = value[n * rows:(n + 1) * rows]
+            slots[h] = piece
+            if k == 0:
+                own[:, cols] = piece
+            else:
+                out.append(send(slots.at[h], own.at[:, cols], s.at[k - 1], r.at[k - 1], head_dev(k)))
+        return out
+
+    def halves(ref, value, n):
+        value = value.reshape(2, H * rows, HD)
+        ref[...] = value if n == 0 else ref[...] + value
+
+    at_copies = []
+    for n, ks in enumerate(blocks):
+        score = contract_cols(stacked(q_buf, ks), keys) * scale
         score = score + jnp.concatenate(
             [
                 jnp.broadcast_to(bias[pl.ds(h * spans + s, 1), :], (SPAN, width))
-                for s in range(spans)
+                for h in slots_of(ks) for s in range(spans)
             ],
             axis=0,
         )
         prob = jnp.exp(score - jnp.max(score, axis=1, keepdims=True))
         prob = prob * (1.0 / jnp.sum(prob, axis=1, keepdims=True))
+        p_buf[n] = prob
         prob_b = prob.astype(bf)
-        att = dot_plain(prob_b, values).astype(bf)
-        att_send[h] = att
-        if k == 0:
-            att_own[:, cols] = att
-        else:
-            at_copies.append(send(
-                att_send.at[h], att_own.at[:, cols], at_s.at[k - 1], at_r.at[k - 1], head_dev(k)
-            ))
-        d_prob = contract_cols(grad, values)
+        at_copies += deal(dot_plain(prob_b, values).astype(bf), ks, att_send, att_own, at_s, at_r)
+        halves(dv_acc, dot_rows(prob_b, stacked(g_got, ks)), n)
+    pair_dv = send(dv_acc.at[other], dv_pair, pair_s.at[0], pair_r.at[0], pair_dev)
+
+    dq_copies = []
+
+    def backward(n):
+        ks = blocks[n]
+        d_prob = contract_cols(stacked(g_got, ks), values)
+        prob = p_buf[n]
         delta = jnp.sum(prob * d_prob, axis=1, keepdims=True)
         d_score = (prob * (d_prob - delta) * scale).astype(bf)
         d_query = dot_plain(d_score, keys).astype(bf)
-        dq_send[h] = d_query
-        if k == 0:
-            dq_own[:, cols] = d_query
-        else:
-            dq_copies.append(send(
-                dq_send.at[h], dq_own.at[:, cols], dq_s.at[k - 1], dq_r.at[k - 1], head_dev(k)
-            ))
-        d_key = dot_rows(d_score, query).reshape(2, H * rows, HD)
-        d_value = dot_rows(prob_b, grad).reshape(2, H * rows, HD)
-        if k == 1:
-            dkv_acc[:, :, :HD] = d_key
-            dkv_acc[:, :, HD:] = d_value
-        else:
-            dkv_acc[:, :, :HD] += d_key
-            dkv_acc[:, :, HD:] += d_value
-
-    for i in (3, 1, 2):
-        late += w_forward(i)
-    pair_dkv = send(dkv_acc.at[other], dkv_pair, pair_s.at[0], pair_r.at[0], pair_dev)
-
-    for copy in at_copies:
-        copy.wait_recv()
-    attention = att_own[...]
-    part = dot_rows(attention, dy_own[...]).reshape(F, H, 2, -1, dy_own.shape[1])
-    for j in range(2):
-        go0[j] = part[:, :, j].astype(bf)
-    pair_go = send(go0.at[other], go0_got, pair_s.at[1], pair_r.at[1], pair_dev)
-
-    pair_dkv.wait_recv()
-    dkv = (dkv_acc[c] + dkv_pair[...]).astype(bf)
-    for h in range(H):
-        dkv_send[h] = dkv[h * rows:(h + 1) * rows]
-        d_head[h * rows:(h + 1) * rows, :HD] = dq_send[h]
-    d_head[:, HD:] = dkv
-    dk_copies = []
-    for k in range(1, H):
-        to = lax.rem(z + k, H)
-        dk_copies.append(send(
-            dkv_send.at[to], dkv_own.at[z], dk_s.at[k - 1], dk_r.at[k - 1], head_dev(k)
-        ))
-    dkv_own[z] = dkv_send[z]
-
-    part = dot_rows(xg[c].reshape(H * rows, -1), d_head[...]).reshape(F, H, 2, -1, 3 * HD)
-    for j in range(2):
-        gw0[j] = part[:, :, j].astype(bf)
-    pair_gw = send(gw0.at[other], gw0_got, pair_s.at[2], pair_r.at[2], pair_dev)
+        halves(dk_acc, dot_rows(d_score, stacked(q_buf, ks)), n)
+        return deal(d_query, ks, dq_send, dq_own, dq_s, dq_r)
+
+    def finish(acc, pair, copy, slots, own, s, r):
+        copy.wait_recv()
+        total = (acc[c] + pair[...]).astype(bf)
+        for h in range(H):
+            slots[h] = total[h * rows:(h + 1) * rows]
+        own[:, cols] = slots[z]
+        return total, [
+            send(
+                slots.at[lax.rem(z + k, H)], own.at[:, cols], s.at[k - 1], r.at[k - 1], head_dev(k)
+            )
+            for k in range(1, H)
+        ]
+
+    def split(ref, value, at=None):
+        value = value.reshape(F, H, 2, -1, value.shape[1])
+        for j in range(2):
+            if at is None:
+                ref[j] = value[:, :, j].astype(bf)
+            else:
+                ref[j, :, :, :, at * HD:(at + 1) * HD] = value[:, :, j].astype(bf)
 
     def over_clips(kept, got, out, slots, s, r):
         out[...] = (kept[c].astype(f32) + got[...].astype(f32)).astype(bf)
@@ -515,47 +517,65 @@
             total = total + slots[k - 1].astype(f32)
         return total.astype(bf)
 
+    dq_copies += backward(0)
+    for copy in at_copies:
+        copy.wait_recv()
+    attention = att_own[...]
+    split(go0, dot_rows(attention, dy_own[...]))
+    pair_go = send(go0.at[other], go0_got, pair_s.at[1], pair_r.at[1], pair_dev)
+    d_value, dv_copies = finish(dv_acc, dv_pair, pair_dv, dv_send, dv_own, dv_s, dv_r)
+    late = []
+    for i in (1, 2, 3):
+        late += w_forward(i)
+    dq_copies += backward(1)
+    pair_dk = send(dk_acc.at[other], dk_pair, pair_s.at[2], pair_r.at[2], pair_dev)
+
+    split(gv0, dot_plain(xt[...], d_value))
+    pair_gv = send(gv0.at[other], gv0_got, pair_s.at[3], pair_r.at[3], pair_dev)
     pair_go.wait_recv()
     go_copies = over_clips(go0, go0_got, go1, go1_got, go1_s, go1_r)
+    split(gw0, dot_plain(xt[...], dq_send[...].reshape(H * rows, HD)), 0)
+    d_key, dk_copies = finish(dk_acc, dk_pair, pair_dk, dk_send, dk_own, dk_s, dk_r)
+    split(gw0, dot_plain(xt[...], d_key), 1)
+    pair_gw = send(gw0.at[other], gw0_got, pair_s.at[4], pair_r.at[4], pair_dev)
+    pair_gv.wait_recv()
+    gv_copies = over_clips(gv0, gv0_got, gv1, gv1_got, gv1_s, gv1_r)
     mixed_ref[...] = (xg[c, z].astype(f32) + dot_plain(attention, wo_all[...])).astype(bf)
     pair_gw.wait_recv()
     gw_copies = over_clips(gw0, gw0_got, gw1, gw1_got, gw1_s, gw1_r)
 
-    for copy in dq_copies:
-        copy.wait_recv()
-    for copy in late:
-        copy.wait_recv()
-    token = dy_own[...].astype(f32) + contract_cols(dq_own[...], wq_all[...])
+    for copy in late + dv_copies + dq_copies:
+        copy.wait_recv()
+    token = dy_own[...].astype(f32) + contract_cols(dv_own[...], wv_all[...])
+    token = token + contract_cols(dq_own[...], wq_all[...])
     for copy in dk_copies:
         copy.wait_recv()
-    dk_rows = jnp.concatenate([dkv_own[h][:, :HD] for h in range(H)], axis=1)
-    dv_rows = jnp.concatenate([dkv_own[h][:, HD:] for h in range(H)], axis=1)
-    token = token + contract_cols(dk_rows, wk_all[...]) + contract_cols(dv_rows, wv_all[...])
-    token_ref[...] = token.astype(bf)
+    token_ref[...] = (token + contract_cols(dk_own[...], wk_all[...])).astype(bf)
+
+    def to_owner(ref, got, s, r):
+        got[z] = ref[z]
+        return [
+            send(ref.at[lax.rem(z + k, H)], got.at[z], s.at[k - 1], r.at[k - 1], head_dev(k))
+            for k in range(1, H)
+        ]
 
     go2[...] = summed(go_copies, go1, go1_got)
-    go_last = [
-        send(go2.at[lax.rem(z + k, H)], go2_got.at[k - 1], go2_s.at[k - 1], go2_r.at[k - 1], head_dev(k))
-        for k in range(1, H)
-    ]
+    last = to_owner(go2, go2_got, go2_s, go2_r)
+    gv2[...] = summed(gv_copies, gv1, gv1_got)
+    last += to_owner(gv2, gv2_got, gv2_s, gv2_r)
     gw2[...] = summed(gw_copies, gw1, gw1_got)
-    gw_last = [
-        send(gw2.at[lax.rem(z + k, H)], gw2_got.at[z], gw2_s.at[k - 1], gw2_r.at[k - 1], head_dev(k))
-        for k in range(1, H)
-    ]
-    gw2_got[z] = gw2[z]
-    total = go2[z].astype(f32)
-    for k in range(1, H):
-        go_last[k - 1].wait_recv()
-        total = total + go2_got[k - 1].astype(f32)
+    last += to_owner(gw2, gw2_got, gw2_s, gw2_r)
+    for copy in last:
+        copy.wait_recv()
+    total = go2_got[0].astype(f32)
+    for h in range(1, H):
+        total = total + go2_got[h].astype(f32)
     go_ref[...] = total
-    for copy in gw_last:
-        copy.wait_recv()
     for h in range(H):
         piece = gw2_got[h].astype(f32)
         gq_ref[:, h * HD:(h + 1) * HD] = piece[:, :HD]
-        gk_ref[:, h * HD:(h + 1) * HD] = piece[:, HD:2 * HD]
-        gv_ref[:, h * HD:(h + 1) * HD] = piece[:, 2 * HD:]
+        gk_ref[:, h * HD:(h + 1) * HD] = piece[:, HD:]
+        gv_ref[:, h * HD:(h + 1) * HD] = gv2_got[h].astype(f32)
     for copy in started:
         copy.wait_send()
     for can_send, can_recv, out, _, pair, _ in flows.values():
@@ -564,13 +584,18 @@
 
 
 def store_kernel(*refs):
-    n = (len(refs) - 1) // 2
-    sems = refs[-1]
-    copies = [pltpu.make_async_copy(refs[i], refs[n + i], sems.at[i]) for i in range(n)]
-    for copy in copies:
-        copy.start()
-    for copy in copies:
-        copy.wait()
+    n = (len(refs) - 2) // 3
+    srcs, outs, held = refs[:n], refs[n:2 * n], refs[2 * n:3 * n]
+    sems_in, sems_out = refs[-2:]
+    loads = [pltpu.make_async_copy(srcs[i], held[i], sems_in.at[i]) for i in range(n)]
+    stores = [pltpu.make_async_copy(held[i], outs[i], sems_out.at[i]) for i in range(n)]
+    for load in loads:
+        load.start()
+    for load, store in zip(loads, stores):
+        load.wait()
+        store.start()
+    for store in stores:
+        store.wait()
 
 
 def fused_body(F, tokens, cotangent, w_query, w_key, w_value, w_out, block_mask, span_order):
@@ -588,19 +613,23 @@
         V((2, H, rows, D), bf), V((rows, D), bf), V((D, HQ), bf), V((D, HQ), bf), V((D, HQ), bf), V((HQ, D), bf),
         V((D, 3 * HD), bf), V((hr // SPAN, 2 * hr), f32), V((H, rows, HD), bf), V((H, rows, HD), bf),
         V((2, H, rows, 2 * HD), bf), V((H, rows, HD), bf),
-        V((H, rows, HD), bf), V((rows, HQ), bf), V((H, rows, HD), bf), V((rows, HQ), bf),
-        V((2, hr, 2 * HD), f32), V((hr, 2 * HD), f32), V((H, rows, 2 * HD), bf),
-        V((H, rows, 2 * HD), bf), V((hr, 3 * HD), bf),
-        V((2, F, H, go_rows, D), bf), V((F, H, go_rows, D), bf), V((F, H, go_rows, D), bf),
-        V((F - 1, H, go_rows, D), bf), V((H, go_rows, D), bf), V((H - 1, go_rows, D), bf),
-        V((2, F, H, gq_rows, 3 * HD), bf), V((F, H, gq_rows, 3 * HD), bf),
-        V((F, H, gq_rows, 3 * HD), bf), V((F - 1, H, gq_rows, 3 * HD), bf),
-        V((H, gq_rows, 3 * HD), bf), V((H, gq_rows, 3 * HD), bf),
     ]
+    for _ in range(4):
+        scratch += [V((H, rows, HD), bf), V((rows, HQ), bf)]
+    scratch.append(V((2, hr // 2, 2 * hr), f32))
+    for _ in range(2):
+        scratch += [V((2, hr, HD), f32), V((hr, HD), f32)]
+    scratch.append(V((D, hr), bf))
+    for n, wide in ((go_rows, D), (gq_rows, HD), (gq_rows, 2 * HD)):
+        scratch += [
+            V((2, F, H, n, wide), bf), V((F, H, n, wide), bf), V((F, H, n, wide), bf),
+            V((F - 1, H, n, wide), bf), V((H, n, wide), bf), V((H, n, wide), bf),
+        ]
     scratch.append(dma((9,)))
+    head, clip = (H - 1,), (F - 1,)
     for shape in (
-        (2, H - 1), (2, H - 1), (4, F - 1), (4, F - 1), (3, F - 1), (3, F - 1), (1,), (H - 1,), (H - 1,), (H - 1,), (H - 1,), (3,),
-        (F - 1,), (H - 1,), (F - 1,), (H - 1,),
+        (2, H - 1), (2, H - 1), (4, F - 1), (4, F - 1), (3, F - 1), (3, F - 1), (1,),
+        head, head, head, head, head, (5,), clip, head, clip, head, clip, head,
     ):
         scratch += [dma(shape), dma(shape)]
     vmem = pl.BlockSpec(memory_space=pltpu.VMEM)
@@ -627,7 +656,7 @@
         out_shape=tuple(jax.ShapeDtypeStruct(r.shape, r.dtype) for r in results),
         in_specs=[pl.BlockSpec(memory_space=pltpu.HBM)] * 6,
         out_specs=tuple([pl.BlockSpec(memory_space=pltpu.HBM)] * 6),
-        scratch_shapes=[dma((6,))],
+        scratch_shapes=[V(r.shape, r.dtype) for r in results] + [dma((6,)), dma((6,))],
         compiler_params=pltpu.CompilerParams(vmem_limit_bytes=60 * 1024 * 1024),
     )(*results)
     return (mixed[None], token[None], gq, gk, gv, go)

time: 84.1 us -> 59.2 us (0.70)
  Pallas kernels: 83.3 us -> 58.4 us
    pallas_call x1, Pallas kernels: 25 us -> 1.92 us  [fused_body(): pl.pallas_call(store_kernel, out_shape=tuple((jax.ShapeDtypeStruct(r.shap...]
    pallas_call x1, Pallas kernels: 58.3 us -> 56.4 us  [fused_body(): pl.pallas_call(functools.partial(fused_kernel, F), out_shape=(jax.ShapeDt...]
where the time goes in v3:
time: 59.2 us; the launch traced here: 59 us
  Pallas kernels  58.4 us (99%)
  between operations  0.64 us (1%)
    pallas_call x1, Pallas kernels, fused_body(): pl.pallas_call(functools.partial(fused_kernel, F), out_shape=(jax.ShapeDt...  56.4 us
    pallas_call x1, Pallas kernels, fused_body(): pl.pallas_call(store_kernel, out_shape=tuple((jax.ShapeDtypeStruct(r.shap...  1.92 us

profile of v3, /device:TPU:0, one launch (start us, length us, event | category | flops | bytes accessed | tf_op | source)
XLA Modules:
  0.0 59.0 jit_solution(7942242943563803628)
XLA Ops:
  0.6 56.4 %shard_map.127 = (bf16[128,1024]{1,0:T(8,128)(2,1)}, bf16[128,1024]{1,0:T(8,128)(2,1)}, f32[32,512]{1,0:T(8,128)}, f32[32,512]{1,0:T(8,128)}, f32[32,512]{1,0:T(8,128)}, /*index=5*/f32[16,1024]{1,0:T(8,128)}) custom-call(bf16[128,1024]{1,0:T(8,128)(2,1)} %bitcast.4, bf16[128,1024]{1,0:T(8,128)(2,1)} %bitcast.5, bf16[256,512]{1,0:T(8,128)(2,1)} %wq_ref.1, ...), custom_call_target="tpu_custom_call" | custom-call | flops 3000000000 | bytes 4000000 | tf_op jit(solution)/shard_map/pallas_call | solution.py:637
  57.1 1.9 %shard_map.128 = (bf16[128,1024]{1,0:T(8,128)(2,1)}, bf16[128,1024]{1,0:T(8,128)(2,1)}, f32[32,512]{1,0:T(8,128)}, f32[32,512]{1,0:T(8,128)}, f32[32,512]{1,0:T(8,128)}, /*index=5*/f32[16,1024]{1,0:T(8,128)}) custom-call(bf16[128,1024]{1,0:T(8,128)(2,1)} %get-tuple-element.18.refs_0_, bf16[128,1024]{1,0:T(8,128)(2,1)} %get-tuple-element.19.refs_1_, ...), custom_call_target="tpu_custom_call" | custom-call | tf_op jit(solution)/shard_map/pallas_call | solution.py:654

commit v4 on v3

--- a/solution.py
+++ b/solution.py
@@ -214,7 +214,7 @@
     mixed_ref, token_ref, gq_ref, gk_ref, gv_ref, go_ref,
     xg, dy_own, wq_all, wk_all, wv_all, wo_all, wh, bias, g_send, g_got, kv_buf, q_buf,
     att_send, att_own, dq_send, dq_own, dk_send, dk_own, dv_send, dv_own,
-    p_buf, dk_acc, dk_pair, dv_acc, dv_pair, xt,
+    p_buf, s_buf, b_buf, dk_acc, dk_pair, dv_acc, dv_pair, xt,
     go0, go0_got, go1, go1_got, go2, go2_got,
     gv0, gv0_got, gv1, gv1_got, gv2, gv2_got,
     gw0, gw0_got, gw1, gw1_got, gw2, gw2_got,
@@ -401,7 +401,7 @@
 
     pass_on(0)
     wo_forwards = w_forward(0)
-    for i in range(1, 4):
+    for i in (2, 3, 1):
         w_copies[i] = w_send(i)
     for copy in forwards:
         copy.wait_recv()
@@ -454,18 +454,16 @@
 
     at_copies = []
     for n, ks in enumerate(blocks):
-        score = contract_cols(stacked(q_buf, ks), keys) * scale
-        score = score + jnp.concatenate(
-            [
-                jnp.broadcast_to(bias[pl.ds(h * spans + s, 1), :], (SPAN, width))
-                for h in slots_of(ks) for s in range(spans)
-            ],
-            axis=0,
-        )
-        prob = jnp.exp(score - jnp.max(score, axis=1, keepdims=True))
-        prob = prob * (1.0 / jnp.sum(prob, axis=1, keepdims=True))
-        p_buf[n] = prob
-        prob_b = prob.astype(bf)
+        s_buf[...] = contract_cols(stacked(q_buf, ks), keys)
+        lines = [bias[pl.ds(h * spans + s, 1), :] for h in slots_of(ks) for s in range(spans)]
+        for start in range(0, s_buf.shape[0], 16):
+            now = slice(start, start + 16)
+            score = s_buf[now, :] * scale + lines[start // SPAN]
+            prob = jnp.exp(score - jnp.max(score, axis=1, keepdims=True))
+            prob = prob * (1.0 / jnp.sum(prob, axis=1, keepdims=True))
+            p_buf[n, now, :] = prob
+            b_buf[now, :] = prob.astype(bf)
+        prob_b = b_buf[...]
         at_copies += deal(dot_plain(prob_b, values).astype(bf), ks, att_send, att_own, at_s, at_r)
         halves(dv_acc, dot_rows(prob_b, stacked(g_got, ks)), n)
     pair_dv = send(dv_acc.at[other], dv_pair, pair_s.at[0], pair_r.at[0], pair_dev)
@@ -474,10 +472,14 @@
 
     def backward(n):
         ks = blocks[n]
-        d_prob = contract_cols(stacked(g_got, ks), values)
-        prob = p_buf[n]
-        delta = jnp.sum(prob * d_prob, axis=1, keepdims=True)
-        d_score = (prob * (d_prob - delta) * scale).astype(bf)
+        s_buf[...] = contract_cols(stacked(g_got, ks), values)
+        for start in range(0, s_buf.shape[0], 16):
+            now = slice(start, start + 16)
+            prob = p_buf[n, now, :]
+            d_prob = s_buf[now, :]
+            delta = jnp.sum(prob * d_prob, axis=1, keepdims=True)
+            b_buf[now, :] = (prob * (d_prob - delta) * scale).astype(bf)
+        d_score = b_buf[...]
         d_query = dot_plain(d_score, keys).astype(bf)
         halves(dk_acc, dot_rows(d_score, stacked(q_buf, ks)), n)
         return deal(d_query, ks, dq_send, dq_own, dq_s, dq_r)
@@ -524,9 +526,6 @@
     split(go0, dot_rows(attention, dy_own[...]))
     pair_go = send(go0.at[other], go0_got, pair_s.at[1], pair_r.at[1], pair_dev)
     d_value, dv_copies = finish(dv_acc, dv_pair, pair_dv, dv_send, dv_own, dv_s, dv_r)
-    late = []
-    for i in (1, 2, 3):
-        late += w_forward(i)
     dq_copies += backward(1)
     pair_dk = send(dk_acc.at[other], dk_pair, pair_s.at[2], pair_r.at[2], pair_dev)
 
@@ -538,17 +537,20 @@
     d_key, dk_copies = finish(dk_acc, dk_pair, pair_dk, dk_send, dk_own, dk_s, dk_r)
     split(gw0, dot_plain(xt[...], d_key), 1)
     pair_gw = send(gw0.at[other], gw0_got, pair_s.at[4], pair_r.at[4], pair_dev)
+    late = w_forward(2)
     pair_gv.wait_recv()
     gv_copies = over_clips(gv0, gv0_got, gv1, gv1_got, gv1_s, gv1_r)
+    late += w_forward(3)
     mixed_ref[...] = (xg[c, z].astype(f32) + dot_plain(attention, wo_all[...])).astype(bf)
     pair_gw.wait_recv()
     gw_copies = over_clips(gw0, gw0_got, gw1, gw1_got, gw1_s, gw1_r)
 
+    late_key = w_forward(1)
     for copy in late + dv_copies + dq_copies:
         copy.wait_recv()
     token = dy_own[...].astype(f32) + contract_cols(dv_own[...], wv_all[...])
     token = token + contract_cols(dq_own[...], wq_all[...])
-    for copy in dk_copies:
+    for copy in late_key + dk_copies:
         copy.wait_recv()
     token_ref[...] = (token + contract_cols(dk_own[...], wk_all[...])).astype(bf)
 
@@ -616,7 +618,9 @@
     ]
     for _ in range(4):
         scratch += [V((H, rows, HD), bf), V((rows, HQ), bf)]
-    scratch.append(V((2, hr // 2, 2 * hr), f32))
+    scratch += [
+        V((2, hr // 2, 2 * hr), f32), V((hr // 2, 2 * hr), f32), V((hr // 2, 2 * hr), bf),
+    ]
     for _ in range(2):
         scratch += [V((2, hr, HD), f32), V((hr, HD), f32)]
     scratch.append(V((D, hr), bf))

time: 59.2 us -> 59.2 us (level)
  no operation moved by 1% of the time
where the time goes in v4:
time: 59.2 us; the launch traced here: 59 us
  Pallas kernels  58.4 us (99%)
  between operations  0.64 us (1%)
    pallas_call x1, Pallas kernels, fused_body(): pl.pallas_call(functools.partial(fused_kernel, F), out_shape=(jax.ShapeDt...  56.4 us
    pallas_call x1, Pallas kernels, fused_body(): pl.pallas_call(store_kernel, out_shape=tuple((jax.ShapeDtypeStruct(r.shap...  1.92 us

profile of v4, /device:TPU:0, one launch (start us, length us, event | category | flops | bytes accessed | tf_op | source)
XLA Modules:
  0.0 59.0 jit_solution(16836022886617345320)
XLA Ops:
  0.6 56.4 %shard_map.127 = (bf16[128,1024]{1,0:T(8,128)(2,1)}, bf16[128,1024]{1,0:T(8,128)(2,1)}, f32[32,512]{1,0:T(8,128)}, f32[32,512]{1,0:T(8,128)}, f32[32,512]{1,0:T(8,128)}, /*index=5*/f32[16,1024]{1,0:T(8,128)}) custom-call(bf16[128,1024]{1,0:T(8,128)(2,1)} %bitcast.4, bf16[128,1024]{1,0:T(8,128)(2,1)} %bitcast.5, bf16[256,512]{1,0:T(8,128)(2,1)} %wq_ref.1, ...), custom_call_target="tpu_custom_call" | custom-call | flops 3000000000 | bytes 4000000 | tf_op jit(solution)/shard_map/pallas_call | solution.py:641
  57.1 1.9 %shard_map.128 = (bf16[128,1024]{1,0:T(8,128)(2,1)}, bf16[128,1024]{1,0:T(8,128)(2,1)}, f32[32,512]{1,0:T(8,128)}, f32[32,512]{1,0:T(8,128)}, f32[32,512]{1,0:T(8,128)}, /*index=5*/f32[16,1024]{1,0:T(8,128)}) custom-call(bf16[128,1024]{1,0:T(8,128)(2,1)} %get-tuple-element.18.refs_0_, bf16[128,1024]{1,0:T(8,128)(2,1)} %get-tuple-element.19.refs_1_, ...), custom_call_target="tpu_custom_call" | custom-call | tf_op jit(solution)/shard_map/pallas_call | solution.py:658

commit v5 on v4

--- a/solution.py
+++ b/solution.py
@@ -331,6 +331,8 @@
         ]
 
     w_copies = {0: w_send(0)}
+    for i in (2, 3, 1):
+        w_copies[i] = w_send(i)
 
     def w_forward(i):
         out = []
@@ -401,8 +403,6 @@
 
     pass_on(0)
     wo_forwards = w_forward(0)
-    for i in (2, 3, 1):
-        w_copies[i] = w_send(i)
     for copy in forwards:
         copy.wait_recv()
     project_own(z)

time: 59.2 us -> 57.7 us (0.975)
  Pallas kernels: 58.4 us -> 56.9 us
    pallas_call x1, Pallas kernels: 56.4 us -> 54.9 us  [fused_body(): pl.pallas_call(functools.partial(fused_kernel, F), out_shape=(jax.ShapeDt...]
where the time goes in v5:
time: 57.7 us; the launch traced here: 57.5 us
  Pallas kernels  56.9 us (99%)
  between operations  0.64 us (1%)
    pallas_call x1, Pallas kernels, fused_body(): pl.pallas_call(functools.partial(fused_kernel, F), out_shape=(jax.ShapeDt...  54.9 us
    pallas_call x1, Pallas kernels, fused_body(): pl.pallas_call(store_kernel, out_shape=tuple((jax.ShapeDtypeStruct(r.shap...  1.92 us

profile of v5, /device:TPU:0, one launch (start us, length us, event | category | flops | bytes accessed | tf_op | source)
XLA Modules:
  0.0 57.5 jit_solution(14380635639039830355)
XLA Ops:
  0.6 54.9 %shard_map.127 = (bf16[128,1024]{1,0:T(8,128)(2,1)}, bf16[128,1024]{1,0:T(8,128)(2,1)}, f32[32,512]{1,0:T(8,128)}, f32[32,512]{1,0:T(8,128)}, f32[32,512]{1,0:T(8,128)}, /*index=5*/f32[16,1024]{1,0:T(8,128)}) custom-call(bf16[128,1024]{1,0:T(8,128)(2,1)} %bitcast.4, bf16[128,1024]{1,0:T(8,128)(2,1)} %bitcast.5, bf16[256,512]{1,0:T(8,128)(2,1)} %wq_ref.1, ...), custom_call_target="tpu_custom_call" | custom-call | flops 3000000000 | bytes 4000000 | tf_op jit(solution)/shard_map/pallas_call | solution.py:641
  55.6 1.9 %shard_map.128 = (bf16[128,1024]{1,0:T(8,128)(2,1)}, bf16[128,1024]{1,0:T(8,128)(2,1)}, f32[32,512]{1,0:T(8,128)}, f32[32,512]{1,0:T(8,128)}, f32[32,512]{1,0:T(8,128)}, /*index=5*/f32[16,1024]{1,0:T(8,128)}) custom-call(bf16[128,1024]{1,0:T(8,128)(2,1)} %get-tuple-element.18.refs_0_, bf16[128,1024]{1,0:T(8,128)(2,1)} %get-tuple-element.19.refs_1_, ...), custom_call_target="tpu_custom_call" | custom-call | tf_op jit(solution)/shard_map/pallas_call | solution.py:658
